TPU v7x, 32 devices: a whole 2x2x4 slice. The times are simulated.
32 devices in a mesh: band: 4 (over y, x), dev: 8 (over z, core).
Axes of the slice: x: 2, y: 2, z: 4, core: 2. Of those that a mesh axis runs over, the one named last changes fastest.
Arguments:
- drive: float32 [2, 32, 16384], P(None, None, ('band', 'dev')), may hold values from -6 to 6
- coords: float32 [3, 16384], P(None, ('band', 'dev')), may hold values from 0 to 3
- rule_index: int32 [16384], P(('band', 'dev')), may hold values from 0 to 3
- rule_weight: float32 [4], replicated, may hold values from 0.1 to 0.4
- pair_cols: int32 [3072], P(('band', 'dev')), may hold values from 0 to 63, as said below
- pair_count: int32 [32], P(('band', 'dev')), may hold values from 12 to 96, as said below
Outputs:
- near_field: float32 [2, 32, 16384], P(None, None, ('band', 'dev'))
Inputs may be any that keep to these rules, and one draw needn't show every extreme that they name: `pair_cols`: for slot s of device k the listed block column lies from k * 2 + (s mod 2) up to that row plus 16 - 1; slots s < 2 list the diagonal pair. `pair_count`: some device has all 96 slots live.
All inputs are finite; a program needn't handle non-finite values.
Results may differ from a plain program's by a relative error of at most 0.0003.
Values sent between devices are 32-bit elements; how exact they have to be, the bound alone decides.
No kernel may reach another device: no remote copies, remote signals or barrier semaphores. Data moves between devices by JAX's collectives and lax.ppermute only.
A program may use at most 64 MiB of HBM per device.

v0:
```python
import functools
import math

import jax
import jax.numpy as jnp
from jax import lax
from jax.experimental import pallas as pl
from jax.experimental.pallas import tpu as pltpu
from jax.sharding import PartitionSpec as P

BLOCK = 256
STRIP = 16
UNROLL = 2
VMEM_LIMIT = 48 * 1024 * 1024

wave_number = 25.0
smoothing = 0.05
per_unit = wave_number / (2.0 * math.pi)
core_sq = (smoothing * per_unit) ** 2
amplitude = per_unit / (4.0 * math.pi)
TOP = tuple(term / 1.01171596 for term in (3.14155014, -3.02333093))
BOTTOM = tuple(term / 1.01171596 for term in (1.0, -4.25291808))

COUNT_ROW = 3
WEIGHT_ROW = 4
EXTRA = 8


def horner(z, terms):
    value = z * terms[-1] + terms[-2]
    for term in terms[-3::-1]:
        value = value * z + term
    return value


def wave(near, far):
    square = None
    for a, b in zip(near, far):
        gap = a - b
        gap = gap * gap
        square = gap + core_sq if square is None else square + gap
    inverse = lax.rsqrt(square)
    turns = square * inverse
    part = turns - jnp.round(turns)
    z = part * part
    top = horner(z, TOP) * part
    bottom = (z + BOTTOM[1]) * z + BOTTOM[0]
    top_sq, bottom_sq = top * top, bottom * bottom
    scaled = inverse * pl.reciprocal(top_sq + bottom_sq, approx=True)
    return (bottom_sq - top_sq) * scaled, (top * bottom) * scaled


def pack_kernel(width, drive, coords, rules, rule_weight, pair_cols, pair_count, out, extra):
    patterns = drive.shape[1]
    slots = pair_cols.shape[1]
    first_row = (lax.axis_index("band") * lax.axis_size("dev") + lax.axis_index("dev")) * 2
    weight = jnp.zeros(rules.shape, jnp.float32)
    for rule in range(rule_weight.shape[1]):
        weight = jnp.where(rules[...] == rule, rule_weight[0:1, rule : rule + 1], weight)
    scale = weight * amplitude
    out[0:patterns, :] = drive[0] * scale
    out[patterns : 2 * patterns, :] = drive[1] * scale
    slot = lax.broadcasted_iota(jnp.int32, (8, slots), 1)
    odd = lax.rem(slot, 2)
    place = pair_cols[...] - first_row - odd + odd * width
    place = jnp.where(slot < pair_count[...], place, -1).T[:, 0:1]
    lanes = lax.broadcasted_iota(jnp.int32, (slots, 2 * width), 1)
    counts = jnp.sum(jnp.where(lanes == place, 1.0, 0.0), axis=0, keepdims=True)
    base = 2 * patterns
    for ref, first in ((out, base), (extra, 0)):
        ref[first : first + EXTRA, :] = jnp.zeros((EXTRA, out.shape[1]), jnp.float32)
        ref[first : first + 3, :] = coords[...] * per_unit
        ref[first + COUNT_ROW : first + COUNT_ROW + 1, 0 : 2 * width] = counts
        ref[first + WEIGHT_ROW : first + WEIGHT_ROW + 1, :] = weight


def near_kernel(spec, names, *refs):
    ref = dict(zip(names, refs, strict=True))
    blocks, first_block, width, groups, outs, part = (
        spec[k] for k in ("blocks", "first_block", "width", "groups", "outs", "part")
    )
    left, across, acc, points = ref["left"], ref["across"], ref["acc"], ref["points"]
    plan, factor = ref["plan"], ref["factor"]
    own_points = ref["own_points"]
    even = lax.rem(lax.axis_index("band"), 2) == 0
    base = acc.shape[1]
    half = base // 2
    spans = [slice(r * BLOCK, (r + 1) * BLOCK) for r in range(2)]

    copies = []
    if part != "tail":
        tables, sem = ref["tables"], ref["sem"]
        lanes = tables.shape[2]
        sources = [ref["col", s].at[base : base + EXTRA, 0:lanes] for s in range(blocks)]
        sources.append(own_points.at[:, 0:lanes])
        if 1 in groups:
            before = ref["before"]
            before[...] = jnp.where(
                even, ref["points", 1][:, 0:lanes], ref["points", 0][:, 0:lanes]
            )
            sources.append(before)
        copies = [
            pltpu.make_async_copy(source, tables.at[k], sem.at[k])
            for k, source in enumerate(sources)
        ]
        for copy in copies:
            copy.start()
        for s in range(blocks):
            for h, span in enumerate(spans):
                x = ref["col", s][0:base, span]
                turned = jnp.concatenate([-2.0 * x[half:], 2.0 * x[:half]], 0)
                wide = jnp.concatenate([x, turned], 1)
                hi = wide.astype(jnp.bfloat16)
                left[2 * s + h, 0:base, :] = hi
                left[2 * s + h, base : 2 * base, :] = (wide - hi.astype(jnp.float32)).astype(
                    jnp.bfloat16
                )
                across[2 * s + h, :, 0:EXTRA] = ref["col", s][base : base + EXTRA, span].T
    for k, g in enumerate(groups):
        for r, span in enumerate(spans):
            if g in outs:
                if spec["started"]:
                    acc[2 * k + r] = ref["start", g][:, span]
                else:
                    acc[2 * k + r] = jnp.zeros(acc.shape[1:], jnp.float32)
            if g == 0:
                points[2 * k + r] = own_points[:, span]
            elif part != "tail":
                near, far = (0, 1) if g == 1 else (1, 0)
                points[2 * k + r] = jnp.where(
                    even, ref["points", near][:, span], ref["points", far][:, span]
                )
    for copy in copies:
        copy.wait()

    if part == "tail":
        first, end = ref["marks"][0], ref["marks"][1]
    else:
        me = lax.axis_index("dev")
        own_line, before_line = blocks, blocks + 1

        def add(total, s, h, row, value):
            plan[total + 1] = (2 * s + h) * 8 + row
            factor[total + 1] = value
            return total + jnp.where(value > 0.0, 1, 0)

        def column_tiles(total, s, edge):
            if s + first_block == 0:
                for h in range(2):
                    for r in range(2):
                        if edge and r == h:
                            continue
                        gap = r - h
                        if edge:
                            line = before_line if gap > 0 else own_line
                            lane, row = 2 * width - 1, 2 * groups.index(-1 if gap > 0 else 1) + r
                        else:
                            line, row = own_line, 2 * groups.index(0) + r
                            lane = h * width + gap if gap >= 0 else r * width - gap
                        total = add(total, s, h, row, tables[line, COUNT_ROW, lane])
                return total
            ahead = jnp.bitwise_xor(me, s + first_block) - me
            after = ahead > 0
            apart = 2 * jnp.abs(ahead)
            if edge:
                line = jnp.where(after, s, before_line)
                rows = jnp.where(after, 2 * groups.index(1), 2 * groups.index(-1))
                gap, first_is_col = width - apart, after
            else:
                line = jnp.where(after, own_line, s)
                rows = 2 * groups.index(0)
                gap, first_is_col = apart, jnp.logical_not(after)
            for h in range(2):
                for r in range(2):
                    if h == r:
                        lane = h * width + gap
                    else:
                        lane = gap + jnp.where(first_is_col, h * width + r - h, r * width + h - r)
                    total = add(total, s, h, rows + r, tables[line, COUNT_ROW, lane])
            return total

        live = jnp.int32(0)
        if 1 in groups:
            for s in range(blocks):
                live = column_tiles(live, s, True)
        edge_tiles = live
        if 0 in groups:
            for s in range(blocks):
                live = column_tiles(live, s, False)
        plan[0] = 0
        factor[0] = 0.0
        plan[live + 1] = 0
        factor[live + 1] = 0.0
        first, end = 0, live
        if part == "head":
            end = jnp.maximum(edge_tiles, live - spec["keep"])
            ref["marks"][0] = end
            ref["marks"][1] = live

    def entry_of(tile):
        entry = plan[tile + 1]
        return lax.shift_right_logical(entry, 3), jnp.bitwise_and(entry, 7)

    def spread(tile, near_ref):
        col, _ = entry_of(tile)
        for at in range(0, BLOCK, STRIP):
            for k in range(3):
                near_ref[k, at : at + STRIP, :] = jnp.broadcast_to(
                    across[col, at : at + STRIP, k : k + 1], (STRIP, near_ref.shape[2])
                )

    def build(tile, hi_ref, lo_ref, near_ref):
        _, row = entry_of(tile)
        far = [points[row, k : k + 1, :] for k in range(3)]
        times = BLOCK // near_ref.shape[2]
        for at in range(0, BLOCK, STRIP):
            near = [jnp.concatenate([near_ref[k, at : at + STRIP, :]] * times, 1) for k in range(3)]
            for value, begin in zip(wave(near, far), (0, BLOCK)):
                hi = value.astype(jnp.bfloat16)
                hi_ref[begin + at : begin + at + STRIP, :] = hi
                lo_ref[begin + at : begin + at + STRIP, :] = (
                    value - hi.astype(jnp.float32)
                ).astype(jnp.bfloat16)

    def apply(tile, hi_ref, lo_ref):
        col, row = entry_of(tile)
        top = jnp.dot(left[col], hi_ref[...], preferred_element_type=jnp.float32)
        rest = jnp.dot(left[col, 0:base], lo_ref[...], preferred_element_type=jnp.float32)
        acc[row] += factor[tile + 1] * (top[:base] + top[base:] + rest)

    slots = [[ref[kind, k] for kind in ("hi", "lo", "near")] for k in range(2)]

    @pl.when(end > first)
    def _():
        for array in slots[1][:2]:
            array[...] = jnp.zeros(array.shape, array.dtype)
        spread(first, slots[0][2])

        def several(i, carry):
            for k in range(UNROLL):
                tile = first + UNROLL * i + k
                here, there = slots[k % 2], slots[(k + 1) % 2]
                build(tile, *here)
                apply(tile - 1, *there[:2])
                spread(tile + 1, there[2])
            return carry

        count = end - first
        lax.fori_loop(0, count // UNROLL, several, 0)
        done = first + count // UNROLL * UNROLL
        if UNROLL > 2:

            def pair(i, carry):
                for k in range(2):
                    tile = done + 2 * i + k
                    here, there = slots[k % 2], slots[(k + 1) % 2]
                    build(tile, *here)
                    apply(tile - 1, *there[:2])
                    spread(tile + 1, there[2])
                return carry

            lax.fori_loop(0, lax.shift_right_logical(end - done, 1), pair, 0)
        odd = jnp.bitwise_and(count, 1) == 1

        @pl.when(odd)
        def _():
            build(end - 1, *slots[0])
            apply(end - 2, *slots[1][:2])
            apply(end - 1, *slots[0][:2])

        @pl.when(jnp.logical_not(odd))
        def _():
            apply(end - 1, *slots[1][:2])

    for g in outs:
        index = groups.index(g)
        if part == "head" and g != 0:
            index = jnp.where(even, groups.index(-g), index)
        for r, span in enumerate(spans):
            ref["sum", g][:, span] = acc[2 * index + r]


def near_part(part, cols, first_block, width, mine, points, groups, outs, starts, ready=None):
    if ready is None:
        blocks = len(cols)
    else:
        blocks = ready["left"].shape[0] // 2
    base, own = (starts or cols)[0].shape
    if not starts:
        base -= EXTRA
    lanes = -(-2 * width // 128) * 128
    n_rows = 2 * len(groups)
    tiles = blocks * 2 * n_rows
    vmem, smem = (pl.BlockSpec(memory_space=m) for m in (pltpu.VMEM, pltpu.SMEM))
    shared = {
        "left": ((2 * blocks, 2 * base, 2 * BLOCK), jnp.bfloat16, pltpu.VMEM),
        "across": ((2 * blocks, BLOCK, 128), jnp.float32, pltpu.VMEM),
        "plan": ((tiles + 8,), jnp.int32, pltpu.SMEM),
        "factor": ((tiles + 8,), jnp.float32, pltpu.SMEM),
    }
    marks = {"marks": ((2,), jnp.int32, pltpu.SMEM)}
    args, outputs, scratch = {}, {}, {}
    args["own_points"] = (mine, vmem)
    for k, value in enumerate(points):
        args["points", k] = (value, vmem)
    for s, value in enumerate(cols):
        args["col", s] = (value, vmem)
    for g, value in zip(outs, starts):
        args["start", g] = (value, vmem)
    for g in outs:
        outputs["sum", g] = ((base, own), jnp.float32, pltpu.VMEM)
    if part == "head":
        outputs |= shared | marks
    elif part == "tail":
        for name, (_, _, memory) in (shared | marks).items():
            args[name] = (ready[name], vmem if memory == pltpu.VMEM else smem)
    else:
        scratch |= shared
    for k in range(2):
        for kind in ("hi", "lo"):
            scratch[kind, k] = ((2 * BLOCK, BLOCK), jnp.bfloat16, pltpu.VMEM)
        scratch["near", k] = ((3, BLOCK, 128), jnp.float32, pltpu.VMEM)
    scratch["points"] = ((n_rows, EXTRA, BLOCK), jnp.float32, pltpu.VMEM)
    scratch["acc"] = ((n_rows, base, BLOCK), jnp.float32, pltpu.VMEM)
    if part != "tail":
        scratch["before"] = ((EXTRA, lanes), jnp.float32, pltpu.VMEM)
        scratch["tables"] = ((blocks + 2, EXTRA, lanes), jnp.float32, pltpu.SMEM)
    scratch_shapes = [memory(shape, dtype) for shape, dtype, memory in scratch.values()]
    names = [*args, *outputs, *scratch]
    if part != "tail":
        scratch_shapes.append(pltpu.SemaphoreType.DMA((blocks + 2,)))
        names.append("sem")
    spec = dict(
        blocks=blocks,
        first_block=first_block,
        width=width,
        groups=groups,
        outs=outs,
        part=part,
        started=bool(starts),
        keep=3 * blocks,
    )
    results = pl.pallas_call(
        functools.partial(near_kernel, spec, names),
        out_shape=[jax.ShapeDtypeStruct(shape, dtype) for shape, dtype, _ in outputs.values()],
        in_specs=[place for _, place in args.values()],
        out_specs=[vmem if memory == pltpu.VMEM else smem for _, _, memory in outputs.values()],
        scratch_shapes=scratch_shapes,
        compiler_params=pltpu.CompilerParams(vmem_limit_bytes=VMEM_LIMIT),
        cost_estimate=pl.CostEstimate(
            flops=tiles * 6 * 4 * base * BLOCK * BLOCK // 2,
            bytes_accessed=4 * base * own * (blocks + 3),
            transcendentals=tiles * BLOCK * BLOCK,
        ),
    )(*(value for value, _ in args.values()))
    return dict(zip(outputs, results, strict=True))


def paired(value, first):
    count = lax.axis_size("band")
    pairs = [(i, i + 1) for i in range(first, count - 1, 2)]
    return lax.ppermute(value, "band", pairs + [(j, i) for i, j in pairs])


def swapped(value, axis, mask):
    return lax.ppermute(value, axis, [(i, i ^ mask) for i in range(lax.axis_size(axis))])


def body(drive, coords, rule_index, rule_weight, pair_cols, pair_count):
    n_dev = lax.axis_size("dev")
    patterns, own = drive.shape[1:]
    width = n_dev * (own // BLOCK)
    vmem = pl.BlockSpec(memory_space=pltpu.VMEM)
    base = 2 * patterns
    payload, mine = pl.pallas_call(
        functools.partial(pack_kernel, width),
        out_shape=[
            pltpu.VMEM((base + EXTRA, own), jnp.float32),
            pltpu.VMEM((EXTRA, own), jnp.float32),
        ],
        in_specs=[vmem] * 6,
        out_specs=[vmem] * 2,
    )(
        drive,
        coords,
        rule_index[None, :],
        rule_weight[None, :],
        pair_cols[None, :],
        pair_count[None, :],
    )
    partner = swapped(payload, "dev", 1)
    others = [swapped(payload, "dev", mask) for mask in range(2, n_dev, 2)]
    chip = [payload, partner]
    own_sum = near_part("all", chip, 0, width, mine, [], (0,), (0,), [])["sum", 0]
    outgoing, _ = lax.optimization_barrier((mine, partner))
    points = [paired(outgoing, 0), paired(outgoing, 1)]
    points, own_sum = lax.optimization_barrier((points, own_sum))
    edges = near_part("all", chip, 0, width, mine, points, (-1, 1), (-1, 1), [])
    edges = [edges["sum", -1], edges["sum", 1]]
    others, edges = lax.optimization_barrier((others, edges))
    later = []
    for value in others:
        later += [value, swapped(value, "dev", 1)]
    groups = (-1, 1, 0)
    head = near_part("head", later, 2, width, mine, points, groups, groups, [*edges, own_sum])
    arrived = paired(head["sum", -1], 0) + paired(head["sum", 1], 1)
    tail = near_part("tail", [], 2, width, mine, [], groups, (0,), [head["sum", 0]], head)
    total = (tail["sum", 0] + arrived) * mine[WEIGHT_ROW]
    return total.reshape(drive.shape)


def solution(mesh):
    spread = ("band", "dev")
    in_specs = (
        P(None, None, spread),
        P(None, spread),
        P(spread),
        P(),
        P(spread),
        P(spread),
    )
    out_specs = P(None, None, spread)
    return jax.shard_map(body, mesh=mesh, in_specs=in_specs, out_specs=out_specs, check_vma=False)
```

profile of v0, /device:TPU:0, one launch (start us, length us, event | category | flops | bytes accessed | tf_op | source)
XLA Modules:
  0.0 44.5 jit_solution(10934336203446955056)
XLA Ops:
  0.7 1.2 %shard_map.64 = (f32[72,512]{1,0:T(8,128)S(1)}, f32[8,512]{1,0:T(8,128)S(1)}) custom-call(f32[2,32,512]{2,1,0:T(8,128)} %drive.1, f32[3,512]{1,0:T(4,128)} %coords.1, s32[1,512]{1,0:T(1,128)} %bitcast.8, f32[1,4]{1,0:T(1,128)} %bitcast.9, s32[1,96]{1,0:T(1,128)} %bitcast.10, s32[1,1]{1,0:T(1,128)} %bitcast.6.pair_count), custom_call_target="tpu_custom_call" | custom-call | tf_op jit(solution)/shard_map/pallas_call | solution.py:375
  1.8 0.5 %collective-permute-start = (f32[72,512]{1,0:T(8,128)S(1)}, f32[72,512]{1,0:T(8,128)S(1)}, u32[]{:S(2)}, u32[]{:S(2)}) collective-permute-start(f32[72,512]{1,0:T(8,128)S(1)} %get-tuple-element.27.refs_1_.refs_3_), channel_id=1, source_target_pairs={{0,1},{1,0},{2,3},{3,2},{4,5},{5,4},{6,7},{7,6},{8,9},{9,8},{10,11... | collective-permute-start | bytes 442376 | tf_op jit(solution)/shard_map/ppermute | solution.py:366
  2.4 2.6 %collective-permute-start.3 = (f32[72,512]{1,0:T(8,128)S(1)}, f32[72,512]{1,0:T(8,128)S(1)}, u32[]{:S(2)}, u32[]{:S(2)}) collective-permute-start(f32[72,512]{1,0:T(8,128)S(1)} %get-tuple-element.27.refs_1_.refs_3_), channel_id=1, source_target_pairs={{0,2},{1,3},{2,0},{3,1},{4,6},{5,7},{6,4},{7,5},{8,10},{9,11},{10,... | collective-permute-start | bytes 442376 | tf_op jit(solution)/shard_map/ppermute | solution.py:366
  5.0 2.6 %collective-permute-start.4 = (f32[72,512]{1,0:T(8,128)S(1)}, f32[72,512]{1,0:T(8,128)S(1)}, u32[]{:S(2)}, u32[]{:S(2)}) collective-permute-start(f32[72,512]{1,0:T(8,128)S(1)} %get-tuple-element.27.refs_1_.refs_3_), channel_id=1, source_target_pairs={{0,4},{1,5},{2,6},{3,7},{4,0},{5,1},{6,2},{7,3},{8,12},{9,13},{10,... | collective-permute-start | bytes 442376 | tf_op jit(solution)/shard_map/ppermute | solution.py:366
  7.6 0.0 collective-permute-start.5
  7.6 0.0 collective-permute-done.refs_2_.refs_4_
  7.6 1.7 %collective-permute-start.1 = (f32[8,512]{1,0:T(8,128)S(1)}, f32[8,512]{1,0:T(8,128)S(1)}, u32[]{:S(2)}, u32[]{:S(2)}) collective-permute-start(f32[8,512]{1,0:T(8,128)S(1)} %get-tuple-element.28.refs_0_), channel_id=1, source_target_pairs={{0,8},{16,24},{8,0},{24,16},{1,9},{17,25},{9,1},{25,17},{2,10},{18... | collective-permute-start | bytes 49160 | tf_op jit(solution)/shard_map/ppermute | solution.py:362
  9.3 0.7 %collective-permute-start.2 = (f32[8,512]{1,0:T(8,128)S(1)}, f32[8,512]{1,0:T(8,128)S(1)}, u32[]{:S(2)}, u32[]{:S(2)}) collective-permute-start(f32[8,512]{1,0:T(8,128)S(1)} %get-tuple-element.28.refs_0_), channel_id=1, source_target_pairs={{8,16},{16,8},{9,17},{17,9},{10,18},{18,10},{11,19},{19,11},{12,20... | collective-permute-start | bytes 49160 | tf_op jit(solution)/shard_map/ppermute | solution.py:362
  10.0 3.8 %shard_map.65.refs_11_ = f32[64,512]{1,0:T(8,128)S(1)} custom-call(f32[8,512]{1,0:T(8,128)S(1)} %get-tuple-element.28.refs_0_, f32[72,512]{1,0:T(8,128)S(1)} %get-tuple-element.27.refs_1_.refs_3_, f32[72,512]{1,0:T(8,128)S(1)} %collective-permute-done.refs_2_.refs_4_), custom_call_target="tpu_custom_call" | custom-call | flops 402653184 | bytes 655360 | tf_op jit(solution)/shard_map/pallas_call | solution.py:343
  13.8 0.0 collective-permute-done.1.refs_1_
  13.8 0.0 collective-permute-done.2.refs_2_
  13.8 1.6 %shard_map.66 = (f32[64,512]{1,0:T(8,128)S(1)}, f32[64,512]{1,0:T(8,128)S(1)}) custom-call(f32[8,512]{1,0:T(8,128)S(1)} %get-tuple-element.28.refs_0_, f32[8,512]{1,0:T(8,128)S(1)} %collective-permute-done.1.refs_1_, f32[8,512]{1,0:T(8,128)S(1)} %collective-permute-done.2.refs_2_, f32[72,512]{1,0:T(8,128)S(1)} %get-tuple-element.27.refs_1_.refs_3_, ...), custom_call_target="tpu_custom_call" | custom-call | flops 805306368 | bytes 655360 | tf_op jit(solution)/shard_map/pallas_call | solution.py:343
  15.4 0.0 collective-permute-done.3.refs_3_
  15.5 3.5 %collective-permute-done.4.refs_5_ = f32[72,512]{1,0:T(8,128)S(1)} collective-permute-done((f32[72,512]{1,0:T(8,128)S(1)}, f32[72,512]{1,0:T(8,128)S(1)}, u32[]{:S(2)}, u32[]{:S(2)}) %collective-permute-start.4) | collective-permute-done | bytes 147488 | tf_op jit(solution)/shard_map/ppermute | solution.py:366
  19.0 0.0 collective-permute-done.5.refs_7_
  19.0 0.0 collective-permute-start.6
  19.0 0.5 %collective-permute-start.7 = (f32[72,512]{1,0:T(8,128)S(1)}, f32[72,512]{1,0:T(8,128)S(1)}, u32[]{:S(2)}, u32[]{:S(2)}) collective-permute-start(f32[72,512]{1,0:T(8,128)S(1)} %collective-permute-done.4.refs_5_), channel_id=1, source_target_pairs={{0,1},{1,0},{2,3},{3,2},{4,5},{5,4},{6,7},{7,6},{8,9},{9,8},{10,11... | collective-permute-start | bytes 442376 | tf_op jit(solution)/shard_map/ppermute | solution.py:366
  19.5 0.0 collective-permute-start.8
  19.5 0.9 %collective-permute-done.6.refs_4_ = f32[72,512]{1,0:T(8,128)S(1)} collective-permute-done((f32[72,512]{1,0:T(8,128)S(1)}, f32[72,512]{1,0:T(8,128)S(1)}, u32[]{:S(2)}, u32[]{:S(2)}) %collective-permute-start.6) | collective-permute-done | bytes 147488 | tf_op jit(solution)/shard_map/ppermute | solution.py:366
  20.4 0.2 collective-permute-done.7.refs_6_
  20.6 0.3 collective-permute-done.8.refs_8_
  20.9 8.5 %shard_map.67 = (f32[64,512]{1,0:T(8,128)S(1)}, f32[64,512]{1,0:T(8,128)S(1)}, f32[64,512]{1,0:T(8,128)S(1)}, bf16[12,128,512]{2,1,0:T(8,128)(2,1)S(1)}, f32[12,...) custom-call(f32[8,512]{1,0:T(8,128)S(1)} %get-tuple-element.28.refs_0_, ...), custom_call_target="tpu_custom_call" | custom-call | flops 3623878656 | bytes 1179648 | tf_op jit(solution)/shard_map/pallas_call | solution.py:343
  29.4 0.7 %collective-permute-start.10 = (f32[64,512]{1,0:T(8,128)S(1)}, f32[64,512]{1,0:T(8,128)S(1)}, u32[]{:S(2)}, u32[]{:S(2)}) collective-permute-start(f32[64,512]{1,0:T(8,128)S(1)} %get-tuple-element.46), channel_id=1, source_target_pairs={{8,16},{16,8},{9,17},{17,9},{10,18},{18,10},{11,19},{19,11},{12,20... | collective-permute-start | bytes 393224 | tf_op jit(solution)/shard_map/ppermute | solution.py:362
  30.0 5.9 %collective-permute-start.9 = (f32[64,512]{1,0:T(8,128)S(1)}, f32[64,512]{1,0:T(8,128)S(1)}, u32[]{:S(2)}, u32[]{:S(2)}) collective-permute-start(f32[64,512]{1,0:T(8,128)S(1)} %get-tuple-element.45), channel_id=1, source_target_pairs={{0,8},{16,24},{8,0},{24,16},{1,9},{17,25},{9,1},{25,17},{2,10},{18... | collective-permute-start | bytes 393224 | tf_op jit(solution)/shard_map/ppermute | solution.py:362
  35.9 7.8 %shard_map.68 = f32[64,512]{1,0:T(8,128)S(1)} custom-call(f32[8,512]{1,0:T(8,128)S(1)} %get-tuple-element.28.refs_0_, f32[64,512]{1,0:T(8,128)S(1)} %get-tuple-element.39.refs_1_, bf16[12,128,512]{2,1,0:T(8,128)(2,1)S(1)} %get-tuple-element.40.refs_2_, f32[12,256,128]{2,1,0:T(8,128)S(1)} %get-tuple-element.41.refs_3_, s32[80]{0:T(128)S(1)} %get-tuple-element.42.refs_4_, ...), custom_call_target="tpu_custom_call" | custom-call | flops 3623878656 | bytes 1179648 | tf_op jit(solution)/shard_map/pallas_call | solution.py:343
  43.8 0.0 collective-permute-done.10
  43.8 0.0 collective-permute-done.9
  43.8 0.7 %add_multiply_fusion = f32[64,512]{1,0:T(8,128)} fusion(f32[64,512]{1,0:T(8,128)S(1)} %shard_map.68, f32[64,512]{1,0:T(8,128)S(1)} %collective-permute-done.9, f32[64,512]{1,0:T(8,128)S(1)} %collective-permute-done.10, f32[512]{0:T(512)S(1)} %bitcast.7), kind=kLoop, calls=%fused_computation | loop fusion | flops 98304 | bytes 526336 | tf_op jit(solution)/shard_map/mul | solution.py:408
  (1 shorter events, 0.0 us)
Async XLA Ops:
  1.8 5.8 %collective-permute-start = (f32[72,512]{1,0:T(8,128)S(1)}, f32[72,512]{1,0:T(8,128)S(1)}, u32[]{:S(2)}, u32[]{:S(2)}) collective-permute-start(f32[72,512]{1,0:T(8,128)S(1)} %get-tuple-element.27.refs_1_.refs_3_), channel_id=1, source_target_pairs={{0,1},{1,0},{2,3},{3,2},{4,5},{5,4},{6,7},{7,6},{8,9},{9,8},{10,11... | collective-permute-start | bytes 442376 | tf_op jit(solution)/shard_map/ppermute | solution.py:366
  2.4 13.1 %collective-permute-start.3 = (f32[72,512]{1,0:T(8,128)S(1)}, f32[72,512]{1,0:T(8,128)S(1)}, u32[]{:S(2)}, u32[]{:S(2)}) collective-permute-start(f32[72,512]{1,0:T(8,128)S(1)} %get-tuple-element.27.refs_1_.refs_3_), channel_id=1, source_target_pairs={{0,2},{1,3},{2,0},{3,1},{4,6},{5,7},{6,4},{7,5},{8,10},{9,11},{10,... | collective-permute-start | bytes 442376 | tf_op jit(solution)/shard_map/ppermute | solution.py:366
  5.0 14.0 %collective-permute-start.4 = (f32[72,512]{1,0:T(8,128)S(1)}, f32[72,512]{1,0:T(8,128)S(1)}, u32[]{:S(2)}, u32[]{:S(2)}) collective-permute-start(f32[72,512]{1,0:T(8,128)S(1)} %get-tuple-element.27.refs_1_.refs_3_), channel_id=1, source_target_pairs={{0,4},{1,5},{2,6},{3,7},{4,0},{5,1},{6,2},{7,3},{8,12},{9,13},{10,... | collective-permute-start | bytes 442376 | tf_op jit(solution)/shard_map/ppermute | solution.py:366
  7.6 11.4 %collective-permute-start.5 = (f32[72,512]{1,0:T(8,128)S(1)}, f32[72,512]{1,0:T(8,128)S(1)}, u32[]{:S(2)}, u32[]{:S(2)}) collective-permute-start(f32[72,512]{1,0:T(8,128)S(1)} %get-tuple-element.27.refs_1_.refs_3_), channel_id=1, source_target_pairs={{0,6},{1,7},{2,4},{3,5},{4,2},{5,3},{6,0},{7,1},{8,14},{9,15},{10,... | collective-permute-start | bytes 442376 | tf_op jit(solution)/shard_map/ppermute | solution.py:366
  7.6 6.2 %collective-permute-start.1 = (f32[8,512]{1,0:T(8,128)S(1)}, f32[8,512]{1,0:T(8,128)S(1)}, u32[]{:S(2)}, u32[]{:S(2)}) collective-permute-start(f32[8,512]{1,0:T(8,128)S(1)} %get-tuple-element.28.refs_0_), channel_id=1, source_target_pairs={{0,8},{16,24},{8,0},{24,16},{1,9},{17,25},{9,1},{25,17},{2,10},{18... | collective-permute-start | bytes 49160 | tf_op jit(solution)/shard_map/ppermute | solution.py:362
  9.3 4.5 %collective-permute-start.2 = (f32[8,512]{1,0:T(8,128)S(1)}, f32[8,512]{1,0:T(8,128)S(1)}, u32[]{:S(2)}, u32[]{:S(2)}) collective-permute-start(f32[8,512]{1,0:T(8,128)S(1)} %get-tuple-element.28.refs_0_), channel_id=1, source_target_pairs={{8,16},{16,8},{9,17},{17,9},{10,18},{18,10},{11,19},{19,11},{12,20... | collective-permute-start | bytes 49160 | tf_op jit(solution)/shard_map/ppermute | solution.py:362
  19.0 1.4 %collective-permute-start.6 = (f32[72,512]{1,0:T(8,128)S(1)}, f32[72,512]{1,0:T(8,128)S(1)}, u32[]{:S(2)}, u32[]{:S(2)}) collective-permute-start(f32[72,512]{1,0:T(8,128)S(1)} %collective-permute-done.3.refs_3_), channel_id=1, source_target_pairs={{0,1},{1,0},{2,3},{3,2},{4,5},{5,4},{6,7},{7,6},{8,9},{9,8},{10,11... | collective-permute-start | bytes 442376 | tf_op jit(solution)/shard_map/ppermute | solution.py:366
  19.0 1.6 %collective-permute-start.7 = (f32[72,512]{1,0:T(8,128)S(1)}, f32[72,512]{1,0:T(8,128)S(1)}, u32[]{:S(2)}, u32[]{:S(2)}) collective-permute-start(f32[72,512]{1,0:T(8,128)S(1)} %collective-permute-done.4.refs_5_), channel_id=1, source_target_pairs={{0,1},{1,0},{2,3},{3,2},{4,5},{5,4},{6,7},{7,6},{8,9},{9,8},{10,11... | collective-permute-start | bytes 442376 | tf_op jit(solution)/shard_map/ppermute | solution.py:366
  19.5 1.4 %collective-permute-start.8 = (f32[72,512]{1,0:T(8,128)S(1)}, f32[72,512]{1,0:T(8,128)S(1)}, u32[]{:S(2)}, u32[]{:S(2)}) collective-permute-start(f32[72,512]{1,0:T(8,128)S(1)} %collective-permute-done.5.refs_7_), channel_id=1, source_target_pairs={{0,1},{1,0},{2,3},{3,2},{4,5},{5,4},{6,7},{7,6},{8,9},{9,8},{10,11... | collective-permute-start | bytes 442376 | tf_op jit(solution)/shard_map/ppermute | solution.py:366
  29.4 14.4 %collective-permute-start.10 = (f32[64,512]{1,0:T(8,128)S(1)}, f32[64,512]{1,0:T(8,128)S(1)}, u32[]{:S(2)}, u32[]{:S(2)}) collective-permute-start(f32[64,512]{1,0:T(8,128)S(1)} %get-tuple-element.46), channel_id=1, source_target_pairs={{8,16},{16,8},{9,17},{17,9},{10,18},{18,10},{11,19},{19,11},{12,20... | collective-permute-start | bytes 393224 | tf_op jit(solution)/shard_map/ppermute | solution.py:362
  30.0 13.7 %collective-permute-start.9 = (f32[64,512]{1,0:T(8,128)S(1)}, f32[64,512]{1,0:T(8,128)S(1)}, u32[]{:S(2)}, u32[]{:S(2)}) collective-permute-start(f32[64,512]{1,0:T(8,128)S(1)} %get-tuple-element.45), channel_id=1, source_target_pairs={{0,8},{16,24},{8,0},{24,16},{1,9},{17,25},{9,1},{25,17},{2,10},{18... | collective-permute-start | bytes 393224 | tf_op jit(solution)/shard_map/ppermute | solution.py:362
where the time goes:
time: 45 us; the launch traced here: 44.5 us
  Pallas kernels  22.9 us (51%)
  starting transfers between devices  15.2 us (34%)
  waiting for transfers between devices  4.9 us (11%)
  between operations  0.76 us (2%)
  other arithmetic  0.69 us (2%)
    pallas_call x4, Pallas kernels, near_part(): pl.pallas_call(functools.partial(near_kernel, spec, names), out_shape=[ja...  21.8 us
    ppermute x4, starting transfers between devices, paired(): return lax.ppermute(value, 'band', pairs + [(j, i) for i, j in pairs])  8.9 us
    ppermute x7, starting transfers between devices, swapped(): lax.ppermute(value, axis, [(i, i ^ mask) for i in range(lax.axis_size(axi...  6.27 us
    ppermute x7, waiting for transfers between devices, swapped(): lax.ppermute(value, axis, [(i, i ^ mask) for i in range(lax.axis_size(axi...  4.89 us
    pallas_call x1, Pallas kernels, body(): pl.pallas_call(functools.partial(pack_kernel, width), out_shape=[pltpu.VM...  1.19 us
  transfers between devices with their start and end apart: 11, of which 4 were waited for; matrix products, arithmetic and copies ran while one was open for 0% of the time, Pallas kernels for 30%

commit v1 on v0

--- a/solution.py
+++ b/solution.py
@@ -11,6 +11,8 @@
 BLOCK = 256
 STRIP = 16
 UNROLL = 2
+FILL = 16
+FILL_LAST = 17
 VMEM_LIMIT = 48 * 1024 * 1024
 
 wave_number = 25.0
@@ -119,7 +121,7 @@
     for k, g in enumerate(groups):
         for r, span in enumerate(spans):
             if g in outs:
-                if spec["started"]:
+                if ("start", g) in ref:
                     acc[2 * k + r] = ref["start", g][:, span]
                 else:
                     acc[2 * k + r] = jnp.zeros(acc.shape[1:], jnp.float32)
@@ -185,7 +187,7 @@
                 live = column_tiles(live, s, True)
         edge_tiles = live
         if 0 in groups:
-            for s in range(blocks):
+            for s in range(spec["own_done"], blocks):
                 live = column_tiles(live, s, False)
         plan[0] = 0
         factor[0] = 0.0
@@ -193,7 +195,11 @@
         factor[live + 1] = 0.0
         first, end = 0, live
         if part == "head":
-            end = jnp.maximum(edge_tiles, live - spec["keep"])
+            band, bands = lax.axis_index("band"), lax.axis_size("band")
+            last = (band == 0) | (band == bands - 1)
+            fill = jnp.where(last, spec["fill_last"], spec["fill"])
+            end = jnp.maximum(jnp.minimum(live, fill), live - spec["keep"])
+            end = jnp.maximum(edge_tiles, end)
             ref["marks"][0] = end
             ref["marks"][1] = live
 
@@ -280,14 +286,17 @@
             ref["sum", g][:, span] = acc[2 * index + r]
 
 
-def near_part(part, cols, first_block, width, mine, points, groups, outs, starts, ready=None):
+def near_part(
+    part, cols, first_block, width, mine, points, groups, outs, starts, ready=None, own_done=0
+):
     if ready is None:
         blocks = len(cols)
     else:
         blocks = ready["left"].shape[0] // 2
-    base, own = (starts or cols)[0].shape
-    if not starts:
-        base -= EXTRA
+    if cols:
+        base, own = cols[0].shape[0] - EXTRA, cols[0].shape[1]
+    else:
+        base, own = starts[0].shape
     lanes = -(-2 * width // 128) * 128
     n_rows = 2 * len(groups)
     tiles = blocks * 2 * n_rows
@@ -305,7 +314,7 @@
         args["points", k] = (value, vmem)
     for s, value in enumerate(cols):
         args["col", s] = (value, vmem)
-    for g, value in zip(outs, starts):
+    for g, value in starts.items():
         args["start", g] = (value, vmem)
     for g in outs:
         outputs["sum", g] = ((base, own), jnp.float32, pltpu.VMEM)
@@ -337,8 +346,10 @@
         groups=groups,
         outs=outs,
         part=part,
-        started=bool(starts),
-        keep=3 * blocks,
+        own_done=own_done,
+        keep=13 * blocks // 5,
+        fill=FILL * blocks // 5,
+        fill_last=FILL_LAST * blocks // 5,
     )
     results = pl.pallas_call(
         functools.partial(near_kernel, spec, names),
@@ -391,20 +402,23 @@
     partner = swapped(payload, "dev", 1)
     others = [swapped(payload, "dev", mask) for mask in range(2, n_dev, 2)]
     chip = [payload, partner]
-    own_sum = near_part("all", chip, 0, width, mine, [], (0,), (0,), [])["sum", 0]
+    own_sum = near_part("all", chip, 0, width, mine, [], (0,), (0,), {})["sum", 0]
     outgoing, _ = lax.optimization_barrier((mine, partner))
     points = [paired(outgoing, 0), paired(outgoing, 1)]
     points, own_sum = lax.optimization_barrier((points, own_sum))
-    edges = near_part("all", chip, 0, width, mine, points, (-1, 1), (-1, 1), [])
-    edges = [edges["sum", -1], edges["sum", 1]]
-    others, edges = lax.optimization_barrier((others, edges))
-    later = []
-    for value in others:
+    groups = (-1, 1, 0)
+    cols = chip + others[:1]
+    early = near_part(
+        "all", cols, 0, width, mine, points, groups, groups, {0: own_sum}, own_done=2
+    )
+    sums = {g: early["sum", g] for g in groups}
+    others, sums = lax.optimization_barrier((others, sums))
+    later = [swapped(others[0], "dev", 1)]
+    for value in others[1:]:
         later += [value, swapped(value, "dev", 1)]
-    groups = (-1, 1, 0)
-    head = near_part("head", later, 2, width, mine, points, groups, groups, [*edges, own_sum])
-    arrived = paired(head["sum", -1], 0) + paired(head["sum", 1], 1)
-    tail = near_part("tail", [], 2, width, mine, [], groups, (0,), [head["sum", 0]], head)
+    head = near_part("head", later, len(cols), width, mine, points, groups, groups, sums)
+    arrived = paired(head["sum", 1], 1) + paired(head["sum", -1], 0)
+    tail = near_part("tail", [], 2, width, mine, [], groups, (0,), {0: head["sum", 0]}, head)
     total = (tail["sum", 0] + arrived) * mine[WEIGHT_ROW]
     return total.reshape(drive.shape)
 

time: 45 us -> 41.2 us (0.916)
  the two profiles are of different devices: /device:TPU:0 before, /device:TPU:20 now
where the time goes in v1:
time: 41.2 us; the launch traced here: 40.8 us
  Pallas kernels  24.9 us (60%)
  starting transfers between devices  12.2 us (30%)
  waiting for transfers between devices  2.21 us (5%)
  between operations  0.77 us (2%)
  other arithmetic  0.69 us (2%)
    pallas_call x4, Pallas kernels, near_part(): pl.pallas_call(functools.partial(near_kernel, spec, names), out_shape=[ja...  23.7 us
    ppermute x4, starting transfers between devices, paired(): return lax.ppermute(value, 'band', pairs + [(j, i) for i, j in pairs])  8.08 us
    ppermute x7, starting transfers between devices, swapped(): lax.ppermute(value, axis, [(i, i ^ mask) for i in range(lax.axis_size(axi...  4.14 us
    ppermute x7, waiting for transfers between devices, swapped(): lax.ppermute(value, axis, [(i, i ^ mask) for i in range(lax.axis_size(axi...  2.2 us
    pallas_call x1, Pallas kernels, body(): pl.pallas_call(functools.partial(pack_kernel, width), out_shape=[pltpu.VM...  1.19 us
  transfers between devices with their start and end apart: 11, of which 4 were waited for; matrix products, arithmetic and copies ran while one was open for 0% of the time, Pallas kernels for 36%

profile of v1, /device:TPU:20, one launch (start us, length us, event | category | flops | bytes accessed | tf_op | source)
XLA Modules:
  0.0 40.8 jit_solution(1202089278977481501)
XLA Ops:
  0.7 1.2 %shard_map.64 = (f32[72,512]{1,0:T(8,128)S(1)}, f32[8,512]{1,0:T(8,128)S(1)}) custom-call(f32[2,32,512]{2,1,0:T(8,128)} %drive.1, f32[3,512]{1,0:T(4,128)} %coords.1, s32[1,512]{1,0:T(1,128)} %bitcast.8, f32[1,4]{1,0:T(1,128)} %bitcast.9, s32[1,96]{1,0:T(1,128)} %bitcast.10, s32[1,1]{1,0:T(1,128)} %bitcast.6.pair_count), custom_call_target="tpu_custom_call" | custom-call | tf_op jit(solution)/shard_map/pallas_call | solution.py:386
  1.8 0.1 collective-permute-start
  1.9 1.6 %collective-permute-start.3 = (f32[72,512]{1,0:T(8,128)S(1)}, f32[72,512]{1,0:T(8,128)S(1)}, u32[]{:S(2)}, u32[]{:S(2)}) collective-permute-start(f32[72,512]{1,0:T(8,128)S(1)} %get-tuple-element.29.refs_1_.refs_3_), channel_id=1, source_target_pairs={{0,2},{1,3},{2,0},{3,1},{4,6},{5,7},{6,4},{7,5},{8,10},{9,11},{10,... | collective-permute-start | bytes 442376 | tf_op jit(solution)/shard_map/ppermute | solution.py:377
  3.6 0.3 collective-permute-start.4
  3.9 1.6 %collective-permute-start.5 = (f32[72,512]{1,0:T(8,128)S(1)}, f32[72,512]{1,0:T(8,128)S(1)}, u32[]{:S(2)}, u32[]{:S(2)}) collective-permute-start(f32[72,512]{1,0:T(8,128)S(1)} %get-tuple-element.29.refs_1_.refs_3_), channel_id=1, source_target_pairs={{0,6},{1,7},{2,4},{3,5},{4,2},{5,3},{6,0},{7,1},{8,14},{9,15},{10,... | collective-permute-start | bytes 442376 | tf_op jit(solution)/shard_map/ppermute | solution.py:377
  5.5 0.0 collective-permute-done.refs_2_.refs_4_
  5.5 1.5 %collective-permute-start.1 = (f32[8,512]{1,0:T(8,128)S(1)}, f32[8,512]{1,0:T(8,128)S(1)}, u32[]{:S(2)}, u32[]{:S(2)}) collective-permute-start(f32[8,512]{1,0:T(8,128)S(1)} %get-tuple-element.30.refs_0_), channel_id=1, source_target_pairs={{0,8},{16,24},{8,0},{24,16},{1,9},{17,25},{9,1},{25,17},{2,10},{18... | collective-permute-start | bytes 49160 | tf_op jit(solution)/shard_map/ppermute | solution.py:373
  7.0 2.4 %collective-permute-start.2 = (f32[8,512]{1,0:T(8,128)S(1)}, f32[8,512]{1,0:T(8,128)S(1)}, u32[]{:S(2)}, u32[]{:S(2)}) collective-permute-start(f32[8,512]{1,0:T(8,128)S(1)} %get-tuple-element.30.refs_0_), channel_id=1, source_target_pairs={{8,16},{16,8},{9,17},{17,9},{10,18},{18,10},{11,19},{19,11},{12,20... | collective-permute-start | bytes 49160 | tf_op jit(solution)/shard_map/ppermute | solution.py:373
  9.4 4.2 %shard_map.65.refs_6_ = f32[64,512]{1,0:T(8,128)S(1)} custom-call(f32[8,512]{1,0:T(8,128)S(1)} %get-tuple-element.30.refs_0_, f32[72,512]{1,0:T(8,128)S(1)} %get-tuple-element.29.refs_1_.refs_3_, f32[72,512]{1,0:T(8,128)S(1)} %collective-permute-done.refs_2_.refs_4_), custom_call_target="tpu_custom_call" | custom-call | flops 402653184 | bytes 655360 | tf_op jit(solution)/shard_map/pallas_call | solution.py:354
  13.6 0.0 collective-permute-done.1.refs_1_
  13.6 0.0 collective-permute-done.2.refs_2_
  13.6 0.0 collective-permute-done.3.refs_5_
  13.6 4.4 %shard_map.66 = (f32[64,512]{1,0:T(8,128)S(1)}, f32[64,512]{1,0:T(8,128)S(1)}, f32[64,512]{1,0:T(8,128)S(1)}) custom-call(f32[8,512]{1,0:T(8,128)S(1)} %get-tuple-element.30.refs_0_, f32[8,512]{1,0:T(8,128)S(1)} %collective-permute-done.1.refs_1_, f32[8,512]{1,0:T(8,128)S(1)} %collective-permute-done.2.refs_2_, ...), custom_call_target="tpu_custom_call" | custom-call | flops 1811939328 | bytes 786432 | tf_op jit(solution)/shard_map/pallas_call | solution.py:354
  18.1 0.0 collective-permute-done.4.refs_4_
  18.1 0.8 %collective-permute-done.5.refs_6_ = f32[72,512]{1,0:T(8,128)S(1)} collective-permute-done((f32[72,512]{1,0:T(8,128)S(1)}, f32[72,512]{1,0:T(8,128)S(1)}, u32[]{:S(2)}, u32[]{:S(2)}) %collective-permute-start.5) | collective-permute-done | bytes 147488 | tf_op jit(solution)/shard_map/ppermute | solution.py:377
  18.9 0.0 collective-permute-start.6
  18.9 0.5 %collective-permute-start.7 = (f32[72,512]{1,0:T(8,128)S(1)}, f32[72,512]{1,0:T(8,128)S(1)}, u32[]{:S(2)}, u32[]{:S(2)}) collective-permute-start(f32[72,512]{1,0:T(8,128)S(1)} %collective-permute-done.4.refs_4_), channel_id=1, source_target_pairs={{0,1},{1,0},{2,3},{3,2},{4,5},{5,4},{6,7},{7,6},{8,9},{9,8},{10,11... | collective-permute-start | bytes 442376 | tf_op jit(solution)/shard_map/ppermute | solution.py:377
  19.4 0.0 collective-permute-start.8
  19.4 0.9 %collective-permute-done.6.refs_3_ = f32[72,512]{1,0:T(8,128)S(1)} collective-permute-done((f32[72,512]{1,0:T(8,128)S(1)}, f32[72,512]{1,0:T(8,128)S(1)}, u32[]{:S(2)}, u32[]{:S(2)}) %collective-permute-start.6) | collective-permute-done | bytes 147488 | tf_op jit(solution)/shard_map/ppermute | solution.py:377
  20.3 0.2 collective-permute-done.7.refs_5_
  20.5 0.3 collective-permute-done.8.refs_7_
  20.8 9.2 %shard_map.67 = (f32[64,512]{1,0:T(8,128)S(1)}, f32[64,512]{1,0:T(8,128)S(1)}, f32[64,512]{1,0:T(8,128)S(1)}, bf16[10,128,512]{2,1,0:T(8,128)(2,1)S(1)}, f32[10,...) custom-call(f32[8,512]{1,0:T(8,128)S(1)} %get-tuple-element.30.refs_0_, ...), custom_call_target="tpu_custom_call" | custom-call | flops 3019898880 | bytes 1048576 | tf_op jit(solution)/shard_map/pallas_call | solution.py:354
  29.9 2.3 %collective-permute-start.10 = (f32[64,512]{1,0:T(8,128)S(1)}, f32[64,512]{1,0:T(8,128)S(1)}, u32[]{:S(2)}, u32[]{:S(2)}) collective-permute-start(f32[64,512]{1,0:T(8,128)S(1)} %get-tuple-element.50), channel_id=1, source_target_pairs={{0,8},{16,24},{8,0},{24,16},{1,9},{17,25},{9,1},{25,17},{2,10},{18... | collective-permute-start | bytes 393224 | tf_op jit(solution)/shard_map/ppermute | solution.py:373
  32.3 1.9 %collective-permute-start.9 = (f32[64,512]{1,0:T(8,128)S(1)}, f32[64,512]{1,0:T(8,128)S(1)}, u32[]{:S(2)}, u32[]{:S(2)}) collective-permute-start(f32[64,512]{1,0:T(8,128)S(1)} %get-tuple-element.49), channel_id=1, source_target_pairs={{8,16},{16,8},{9,17},{17,9},{10,18},{18,10},{11,19},{19,11},{12,20... | collective-permute-start | bytes 393224 | tf_op jit(solution)/shard_map/ppermute | solution.py:373
  34.2 5.9 %shard_map.68 = f32[64,512]{1,0:T(8,128)S(1)} custom-call(f32[8,512]{1,0:T(8,128)S(1)} %get-tuple-element.30.refs_0_, f32[64,512]{1,0:T(8,128)S(1)} %get-tuple-element.43.refs_1_, bf16[10,128,512]{2,1,0:T(8,128)(2,1)S(1)} %get-tuple-element.44.refs_2_, f32[10,256,128]{2,1,0:T(8,128)S(1)} %get-tuple-element.45.refs_3_, s32[68]{0:T(128)S(1)} %get-tuple-element.46.refs_4_, ...), custom_call_target="tpu_custom_call" | custom-call | flops 3019898880 | bytes 1048576 | tf_op jit(solution)/shard_map/pallas_call | solution.py:354
  40.1 0.0 collective-permute-done.10
  40.1 0.0 collective-permute-done.9
  40.1 0.7 %add_multiply_fusion = f32[64,512]{1,0:T(8,128)} fusion(f32[64,512]{1,0:T(8,128)S(1)} %shard_map.68, f32[64,512]{1,0:T(8,128)S(1)} %collective-permute-done.9, f32[64,512]{1,0:T(8,128)S(1)} %collective-permute-done.10, f32[512]{0:T(512)S(1)} %bitcast.7), kind=kLoop, calls=%fused_computation | loop fusion | flops 98304 | bytes 526336 | tf_op jit(solution)/shard_map/mul | solution.py:422
  (1 shorter events, 0.0 us)
Async XLA Ops:
  1.8 3.6 %collective-permute-start = (f32[72,512]{1,0:T(8,128)S(1)}, f32[72,512]{1,0:T(8,128)S(1)}, u32[]{:S(2)}, u32[]{:S(2)}) collective-permute-start(f32[72,512]{1,0:T(8,128)S(1)} %get-tuple-element.29.refs_1_.refs_3_), channel_id=1, source_target_pairs={{0,1},{1,0},{2,3},{3,2},{4,5},{5,4},{6,7},{7,6},{8,9},{9,8},{10,11... | collective-permute-start | bytes 442376 | tf_op jit(solution)/shard_map/ppermute | solution.py:377
  1.9 11.7 %collective-permute-start.3 = (f32[72,512]{1,0:T(8,128)S(1)}, f32[72,512]{1,0:T(8,128)S(1)}, u32[]{:S(2)}, u32[]{:S(2)}) collective-permute-start(f32[72,512]{1,0:T(8,128)S(1)} %get-tuple-element.29.refs_1_.refs_3_), channel_id=1, source_target_pairs={{0,2},{1,3},{2,0},{3,1},{4,6},{5,7},{6,4},{7,5},{8,10},{9,11},{10,... | collective-permute-start | bytes 442376 | tf_op jit(solution)/shard_map/ppermute | solution.py:377
  3.6 14.5 %collective-permute-start.4 = (f32[72,512]{1,0:T(8,128)S(1)}, f32[72,512]{1,0:T(8,128)S(1)}, u32[]{:S(2)}, u32[]{:S(2)}) collective-permute-start(f32[72,512]{1,0:T(8,128)S(1)} %get-tuple-element.29.refs_1_.refs_3_), channel_id=1, source_target_pairs={{0,4},{1,5},{2,6},{3,7},{4,0},{5,1},{6,2},{7,3},{8,12},{9,13},{10,... | collective-permute-start | bytes 442376 | tf_op jit(solution)/shard_map/ppermute | solution.py:377
  3.9 15.0 %collective-permute-start.5 = (f32[72,512]{1,0:T(8,128)S(1)}, f32[72,512]{1,0:T(8,128)S(1)}, u32[]{:S(2)}, u32[]{:S(2)}) collective-permute-start(f32[72,512]{1,0:T(8,128)S(1)} %get-tuple-element.29.refs_1_.refs_3_), channel_id=1, source_target_pairs={{0,6},{1,7},{2,4},{3,5},{4,2},{5,3},{6,0},{7,1},{8,14},{9,15},{10,... | collective-permute-start | bytes 442376 | tf_op jit(solution)/shard_map/ppermute | solution.py:377
  5.5 8.1 %collective-permute-start.1 = (f32[8,512]{1,0:T(8,128)S(1)}, f32[8,512]{1,0:T(8,128)S(1)}, u32[]{:S(2)}, u32[]{:S(2)}) collective-permute-start(f32[8,512]{1,0:T(8,128)S(1)} %get-tuple-element.30.refs_0_), channel_id=1, source_target_pairs={{0,8},{16,24},{8,0},{24,16},{1,9},{17,25},{9,1},{25,17},{2,10},{18... | collective-permute-start | bytes 49160 | tf_op jit(solution)/shard_map/ppermute | solution.py:373
  7.0 6.6 %collective-permute-start.2 = (f32[8,512]{1,0:T(8,128)S(1)}, f32[8,512]{1,0:T(8,128)S(1)}, u32[]{:S(2)}, u32[]{:S(2)}) collective-permute-start(f32[8,512]{1,0:T(8,128)S(1)} %get-tuple-element.30.refs_0_), channel_id=1, source_target_pairs={{8,16},{16,8},{9,17},{17,9},{10,18},{18,10},{11,19},{19,11},{12,20... | collective-permute-start | bytes 49160 | tf_op jit(solution)/shard_map/ppermute | solution.py:373
  18.9 1.4 %collective-permute-start.6 = (f32[72,512]{1,0:T(8,128)S(1)}, f32[72,512]{1,0:T(8,128)S(1)}, u32[]{:S(2)}, u32[]{:S(2)}) collective-permute-start(f32[72,512]{1,0:T(8,128)S(1)} %collective-permute-done.3.refs_5_), channel_id=1, source_target_pairs={{0,1},{1,0},{2,3},{3,2},{4,5},{5,4},{6,7},{7,6},{8,9},{9,8},{10,11... | collective-permute-start | bytes 442376 | tf_op jit(solution)/shard_map/ppermute | solution.py:377
  18.9 1.6 %collective-permute-start.7 = (f32[72,512]{1,0:T(8,128)S(1)}, f32[72,512]{1,0:T(8,128)S(1)}, u32[]{:S(2)}, u32[]{:S(2)}) collective-permute-start(f32[72,512]{1,0:T(8,128)S(1)} %collective-permute-done.4.refs_4_), channel_id=1, source_target_pairs={{0,1},{1,0},{2,3},{3,2},{4,5},{5,4},{6,7},{7,6},{8,9},{9,8},{10,11... | collective-permute-start | bytes 442376 | tf_op jit(solution)/shard_map/ppermute | solution.py:377
  19.4 1.4 %collective-permute-start.8 = (f32[72,512]{1,0:T(8,128)S(1)}, f32[72,512]{1,0:T(8,128)S(1)}, u32[]{:S(2)}, u32[]{:S(2)}) collective-permute-start(f32[72,512]{1,0:T(8,128)S(1)} %collective-permute-done.5.refs_6_), channel_id=1, source_target_pairs={{0,1},{1,0},{2,3},{3,2},{4,5},{5,4},{6,7},{7,6},{8,9},{9,8},{10,11... | collective-permute-start | bytes 442376 | tf_op jit(solution)/shard_map/ppermute | solution.py:377
  29.9 10.1 %collective-permute-start.10 = (f32[64,512]{1,0:T(8,128)S(1)}, f32[64,512]{1,0:T(8,128)S(1)}, u32[]{:S(2)}, u32[]{:S(2)}) collective-permute-start(f32[64,512]{1,0:T(8,128)S(1)} %get-tuple-element.50), channel_id=1, source_target_pairs={{0,8},{16,24},{8,0},{24,16},{1,9},{17,25},{9,1},{25,17},{2,10},{18... | collective-permute-start | bytes 393224 | tf_op jit(solution)/shard_map/ppermute | solution.py:373
  32.3 7.9 %collective-permute-start.9 = (f32[64,512]{1,0:T(8,128)S(1)}, f32[64,512]{1,0:T(8,128)S(1)}, u32[]{:S(2)}, u32[]{:S(2)}) collective-permute-start(f32[64,512]{1,0:T(8,128)S(1)} %get-tuple-element.49), channel_id=1, source_target_pairs={{8,16},{16,8},{9,17},{17,9},{10,18},{18,10},{11,19},{19,11},{12,20... | collective-permute-start | bytes 393224 | tf_op jit(solution)/shard_map/ppermute | solution.py:373

commit v2 on v1

--- a/solution.py
+++ b/solution.py
@@ -117,7 +117,13 @@
                 left[2 * s + h, base : 2 * base, :] = (wide - hi.astype(jnp.float32)).astype(
                     jnp.bfloat16
                 )
-                across[2 * s + h, :, 0:EXTRA] = ref["col", s][base : base + EXTRA, span].T
+        lines = [ref["col", s][base : base + EXTRA, span] for s in range(blocks) for span in spans]
+        for k in range(across.shape[0]):
+            some = lines[16 * k : 16 * (k + 1)]
+            spare = 128 - EXTRA * len(some)
+            if spare:
+                some.append(jnp.zeros((spare, BLOCK), jnp.float32))
+            across[k] = jnp.concatenate(some, 0).T
     for k, g in enumerate(groups):
         for r, span in enumerate(spans):
             if g in outs:
@@ -209,10 +215,13 @@
 
     def spread(tile, near_ref):
         col, _ = entry_of(tile)
-        for at in range(0, BLOCK, STRIP):
-            for k in range(3):
-                near_ref[k, at : at + STRIP, :] = jnp.broadcast_to(
-                    across[col, at : at + STRIP, k : k + 1], (STRIP, near_ref.shape[2])
+        group = lax.shift_right_logical(col, 4)
+        lane = EXTRA * jnp.bitwise_and(col, 15)
+        for k in range(3):
+            pick = jnp.full((8, 128), lane + k, jnp.int32)
+            for at in range(0, BLOCK, 8):
+                near_ref[k, at : at + 8, :] = jnp.take_along_axis(
+                    across[group, at : at + 8, :], pick, axis=1, mode="promise_in_bounds"
                 )
 
     def build(tile, hi_ref, lo_ref, near_ref):
@@ -303,7 +312,7 @@
     vmem, smem = (pl.BlockSpec(memory_space=m) for m in (pltpu.VMEM, pltpu.SMEM))
     shared = {
         "left": ((2 * blocks, 2 * base, 2 * BLOCK), jnp.bfloat16, pltpu.VMEM),
-        "across": ((2 * blocks, BLOCK, 128), jnp.float32, pltpu.VMEM),
+        "across": ((-(-blocks // 8), BLOCK, 128), jnp.float32, pltpu.VMEM),
         "plan": ((tiles + 8,), jnp.int32, pltpu.SMEM),
         "factor": ((tiles + 8,), jnp.float32, pltpu.SMEM),
     }

time: 41.2 us -> 41.7 us (1.012)
  the two profiles are of different devices: /device:TPU:20 before, /device:TPU:29 now
where the time goes in v2:
time: 41.7 us; the launch traced here: 42.1 us
  Pallas kernels  25.1 us (60%)
  starting transfers between devices  14 us (34%)
  waiting for transfers between devices  1.6 us (4%)
  between operations  0.76 us (2%)
  other arithmetic  0.69 us (2%)
    pallas_call x4, Pallas kernels, near_part(): pl.pallas_call(functools.partial(near_kernel, spec, names), out_shape=[ja...  23.9 us
    ppermute x4, starting transfers between devices, paired(): return lax.ppermute(value, 'band', pairs + [(j, i) for i, j in pairs])  7.04 us
    ppermute x7, starting transfers between devices, swapped(): lax.ppermute(value, axis, [(i, i ^ mask) for i in range(lax.axis_size(axi...  6.92 us
    pallas_call x1, Pallas kernels, body(): pl.pallas_call(functools.partial(pack_kernel, width), out_shape=[pltpu.VM...  1.19 us
    ppermute x7, waiting for transfers between devices, swapped(): lax.ppermute(value, axis, [(i, i ^ mask) for i in range(lax.axis_size(axi...  1.08 us
  transfers between devices with their start and end apart: 11, of which 4 were waited for; matrix products, arithmetic and copies ran while one was open for 0% of the time, Pallas kernels for 33%

profile of v2, /device:TPU:29, one launch (start us, length us, event | category | flops | bytes accessed | tf_op | source)
XLA Modules:
  0.0 42.1 jit_solution(16668183152756705810)
XLA Ops:
  0.7 1.2 %shard_map.64 = (f32[72,512]{1,0:T(8,128)S(1)}, f32[8,512]{1,0:T(8,128)S(1)}) custom-call(f32[2,32,512]{2,1,0:T(8,128)} %drive.1, f32[3,512]{1,0:T(4,128)} %coords.1, s32[1,512]{1,0:T(1,128)} %bitcast.8, f32[1,4]{1,0:T(1,128)} %bitcast.9, s32[1,96]{1,0:T(1,128)} %bitcast.10, s32[1,1]{1,0:T(1,128)} %bitcast.6.pair_count), custom_call_target="tpu_custom_call" | custom-call | tf_op jit(solution)/shard_map/pallas_call | solution.py:395
  1.8 0.7 %collective-permute-start = (f32[72,512]{1,0:T(8,128)S(1)}, f32[72,512]{1,0:T(8,128)S(1)}, u32[]{:S(2)}, u32[]{:S(2)}) collective-permute-start(f32[72,512]{1,0:T(8,128)S(1)} %get-tuple-element.29.refs_1_.refs_3_), channel_id=1, source_target_pairs={{0,1},{1,0},{2,3},{3,2},{4,5},{5,4},{6,7},{7,6},{8,9},{9,8},{10,11... | collective-permute-start | bytes 442376 | tf_op jit(solution)/shard_map/ppermute | solution.py:386
  2.6 0.2 collective-permute-start.3
  2.8 0.1 collective-permute-start.4
  2.8 3.3 %collective-permute-start.5 = (f32[72,512]{1,0:T(8,128)S(1)}, f32[72,512]{1,0:T(8,128)S(1)}, u32[]{:S(2)}, u32[]{:S(2)}) collective-permute-start(f32[72,512]{1,0:T(8,128)S(1)} %get-tuple-element.29.refs_1_.refs_3_), channel_id=1, source_target_pairs={{0,6},{1,7},{2,4},{3,5},{4,2},{5,3},{6,0},{7,1},{8,14},{9,15},{10,... | collective-permute-start | bytes 442376 | tf_op jit(solution)/shard_map/ppermute | solution.py:386
  6.2 0.0 collective-permute-done.refs_2_.refs_4_
  6.2 1.2 %collective-permute-start.1 = (f32[8,512]{1,0:T(8,128)S(1)}, f32[8,512]{1,0:T(8,128)S(1)}, u32[]{:S(2)}, u32[]{:S(2)}) collective-permute-start(f32[8,512]{1,0:T(8,128)S(1)} %get-tuple-element.30.refs_0_), channel_id=1, source_target_pairs={{0,8},{16,24},{8,0},{24,16},{1,9},{17,25},{9,1},{25,17},{2,10},{18... | collective-permute-start | bytes 49160 | tf_op jit(solution)/shard_map/ppermute | solution.py:382
  7.4 2.1 %collective-permute-start.2 = (f32[8,512]{1,0:T(8,128)S(1)}, f32[8,512]{1,0:T(8,128)S(1)}, u32[]{:S(2)}, u32[]{:S(2)}) collective-permute-start(f32[8,512]{1,0:T(8,128)S(1)} %get-tuple-element.30.refs_0_), channel_id=1, source_target_pairs={{8,16},{16,8},{9,17},{17,9},{10,18},{18,10},{11,19},{19,11},{12,20... | collective-permute-start | bytes 49160 | tf_op jit(solution)/shard_map/ppermute | solution.py:382
  9.5 3.0 %shard_map.65.refs_6_ = f32[64,512]{1,0:T(8,128)S(1)} custom-call(f32[8,512]{1,0:T(8,128)S(1)} %get-tuple-element.30.refs_0_, f32[72,512]{1,0:T(8,128)S(1)} %get-tuple-element.29.refs_1_.refs_3_, f32[72,512]{1,0:T(8,128)S(1)} %collective-permute-done.refs_2_.refs_4_), custom_call_target="tpu_custom_call" | custom-call | flops 402653184 | bytes 655360 | tf_op jit(solution)/shard_map/pallas_call | solution.py:363
  12.5 0.0 collective-permute-done.1.refs_1_
  12.5 0.5 %collective-permute-done.2.refs_2_ = f32[8,512]{1,0:T(8,128)S(1)} collective-permute-done((f32[8,512]{1,0:T(8,128)S(1)}, f32[8,512]{1,0:T(8,128)S(1)}, u32[]{:S(2)}, u32[]{:S(2)}) %collective-permute-start.2) | collective-permute-done | bytes 16416 | tf_op jit(solution)/shard_map/ppermute | solution.py:382
  13.0 0.0 collective-permute-done.3.refs_5_
  13.0 5.2 %shard_map.66 = (f32[64,512]{1,0:T(8,128)S(1)}, f32[64,512]{1,0:T(8,128)S(1)}, f32[64,512]{1,0:T(8,128)S(1)}) custom-call(f32[8,512]{1,0:T(8,128)S(1)} %get-tuple-element.30.refs_0_, f32[8,512]{1,0:T(8,128)S(1)} %collective-permute-done.1.refs_1_, f32[8,512]{1,0:T(8,128)S(1)} %collective-permute-done.2.refs_2_, ...), custom_call_target="tpu_custom_call" | custom-call | flops 1811939328 | bytes 786432 | tf_op jit(solution)/shard_map/pallas_call | solution.py:363
  18.2 0.0 collective-permute-done.4.refs_4_
  18.2 0.0 collective-permute-done.5.refs_6_
  18.2 2.1 %collective-permute-start.6 = (f32[72,512]{1,0:T(8,128)S(1)}, f32[72,512]{1,0:T(8,128)S(1)}, u32[]{:S(2)}, u32[]{:S(2)}) collective-permute-start(f32[72,512]{1,0:T(8,128)S(1)} %collective-permute-done.3.refs_5_), channel_id=1, source_target_pairs={{0,1},{1,0},{2,3},{3,2},{4,5},{5,4},{6,7},{7,6},{8,9},{9,8},{10,11... | collective-permute-start | bytes 442376 | tf_op jit(solution)/shard_map/ppermute | solution.py:386
  20.3 0.1 collective-permute-start.7
  20.4 0.4 %collective-permute-start.8 = (f32[72,512]{1,0:T(8,128)S(1)}, f32[72,512]{1,0:T(8,128)S(1)}, u32[]{:S(2)}, u32[]{:S(2)}) collective-permute-start(f32[72,512]{1,0:T(8,128)S(1)} %collective-permute-done.5.refs_6_), channel_id=1, source_target_pairs={{0,1},{1,0},{2,3},{3,2},{4,5},{5,4},{6,7},{7,6},{8,9},{9,8},{10,11... | collective-permute-start | bytes 442376 | tf_op jit(solution)/shard_map/ppermute | solution.py:386
  20.8 0.5 %collective-permute-done.6.refs_3_ = f32[72,512]{1,0:T(8,128)S(1)} collective-permute-done((f32[72,512]{1,0:T(8,128)S(1)}, f32[72,512]{1,0:T(8,128)S(1)}, u32[]{:S(2)}, u32[]{:S(2)}) %collective-permute-start.6) | collective-permute-done | bytes 147488 | tf_op jit(solution)/shard_map/ppermute | solution.py:386
  21.3 0.4 collective-permute-done.7.refs_5_
  21.7 0.2 collective-permute-done.8.refs_7_
  21.9 9.9 %shard_map.67 = (f32[64,512]{1,0:T(8,128)S(1)}, f32[64,512]{1,0:T(8,128)S(1)}, f32[64,512]{1,0:T(8,128)S(1)}, bf16[10,128,512]{2,1,0:T(8,128)(2,1)S(1)}, f32[1,2...) custom-call(f32[8,512]{1,0:T(8,128)S(1)} %get-tuple-element.30.refs_0_, ...), custom_call_target="tpu_custom_call" | custom-call | flops 3019898880 | bytes 1048576 | tf_op jit(solution)/shard_map/pallas_call | solution.py:363
  31.8 0.1 collective-permute-start.10
  31.9 3.7 %collective-permute-start.9 = (f32[64,512]{1,0:T(8,128)S(1)}, f32[64,512]{1,0:T(8,128)S(1)}, u32[]{:S(2)}, u32[]{:S(2)}) collective-permute-start(f32[64,512]{1,0:T(8,128)S(1)} %get-tuple-element.49), channel_id=1, source_target_pairs={{8,16},{16,8},{9,17},{17,9},{10,18},{18,10},{11,19},{19,11},{12,20... | collective-permute-start | bytes 393224 | tf_op jit(solution)/shard_map/ppermute | solution.py:382
  35.6 5.8 %shard_map.68 = f32[64,512]{1,0:T(8,128)S(1)} custom-call(f32[8,512]{1,0:T(8,128)S(1)} %get-tuple-element.30.refs_0_, f32[64,512]{1,0:T(8,128)S(1)} %get-tuple-element.43.refs_1_, bf16[10,128,512]{2,1,0:T(8,128)(2,1)S(1)} %get-tuple-element.44.refs_2_, f32[1,256,128]{2,1,0:T(8,128)S(1)} %get-tuple-element.45.refs_3_, s32[68]{0:T(128)S(1)} %get-tuple-element.46.refs_4_, ...), custom_call_target="tpu_custom_call" | custom-call | flops 3019898880 | bytes 1048576 | tf_op jit(solution)/shard_map/pallas_call | solution.py:363
  41.4 0.0 collective-permute-done.10
  41.4 0.0 collective-permute-done.9
  41.5 0.7 %add_multiply_fusion = f32[64,512]{1,0:T(8,128)} fusion(f32[64,512]{1,0:T(8,128)S(1)} %shard_map.68, f32[64,512]{1,0:T(8,128)S(1)} %collective-permute-done.9, f32[64,512]{1,0:T(8,128)S(1)} %collective-permute-done.10, f32[512]{0:T(512)S(1)} %bitcast.7), kind=kLoop, calls=%fused_computation | loop fusion | flops 98304 | bytes 526336 | tf_op jit(solution)/shard_map/mul | solution.py:431
  (1 shorter events, 0.0 us)
Async XLA Ops:
  1.8 4.3 %collective-permute-start = (f32[72,512]{1,0:T(8,128)S(1)}, f32[72,512]{1,0:T(8,128)S(1)}, u32[]{:S(2)}, u32[]{:S(2)}) collective-permute-start(f32[72,512]{1,0:T(8,128)S(1)} %get-tuple-element.29.refs_1_.refs_3_), channel_id=1, source_target_pairs={{0,1},{1,0},{2,3},{3,2},{4,5},{5,4},{6,7},{7,6},{8,9},{9,8},{10,11... | collective-permute-start | bytes 442376 | tf_op jit(solution)/shard_map/ppermute | solution.py:386
  2.6 10.4 %collective-permute-start.3 = (f32[72,512]{1,0:T(8,128)S(1)}, f32[72,512]{1,0:T(8,128)S(1)}, u32[]{:S(2)}, u32[]{:S(2)}) collective-permute-start(f32[72,512]{1,0:T(8,128)S(1)} %get-tuple-element.29.refs_1_.refs_3_), channel_id=1, source_target_pairs={{0,2},{1,3},{2,0},{3,1},{4,6},{5,7},{6,4},{7,5},{8,10},{9,11},{10,... | collective-permute-start | bytes 442376 | tf_op jit(solution)/shard_map/ppermute | solution.py:386
  2.8 15.4 %collective-permute-start.4 = (f32[72,512]{1,0:T(8,128)S(1)}, f32[72,512]{1,0:T(8,128)S(1)}, u32[]{:S(2)}, u32[]{:S(2)}) collective-permute-start(f32[72,512]{1,0:T(8,128)S(1)} %get-tuple-element.29.refs_1_.refs_3_), channel_id=1, source_target_pairs={{0,4},{1,5},{2,6},{3,7},{4,0},{5,1},{6,2},{7,3},{8,12},{9,13},{10,... | collective-permute-start | bytes 442376 | tf_op jit(solution)/shard_map/ppermute | solution.py:386
  2.8 15.4 %collective-permute-start.5 = (f32[72,512]{1,0:T(8,128)S(1)}, f32[72,512]{1,0:T(8,128)S(1)}, u32[]{:S(2)}, u32[]{:S(2)}) collective-permute-start(f32[72,512]{1,0:T(8,128)S(1)} %get-tuple-element.29.refs_1_.refs_3_), channel_id=1, source_target_pairs={{0,6},{1,7},{2,4},{3,5},{4,2},{5,3},{6,0},{7,1},{8,14},{9,15},{10,... | collective-permute-start | bytes 442376 | tf_op jit(solution)/shard_map/ppermute | solution.py:386
  6.2 6.3 %collective-permute-start.1 = (f32[8,512]{1,0:T(8,128)S(1)}, f32[8,512]{1,0:T(8,128)S(1)}, u32[]{:S(2)}, u32[]{:S(2)}) collective-permute-start(f32[8,512]{1,0:T(8,128)S(1)} %get-tuple-element.30.refs_0_), channel_id=1, source_target_pairs={{0,8},{16,24},{8,0},{24,16},{1,9},{17,25},{9,1},{25,17},{2,10},{18... | collective-permute-start | bytes 49160 | tf_op jit(solution)/shard_map/ppermute | solution.py:382
  7.4 5.7 %collective-permute-start.2 = (f32[8,512]{1,0:T(8,128)S(1)}, f32[8,512]{1,0:T(8,128)S(1)}, u32[]{:S(2)}, u32[]{:S(2)}) collective-permute-start(f32[8,512]{1,0:T(8,128)S(1)} %get-tuple-element.30.refs_0_), channel_id=1, source_target_pairs={{8,16},{16,8},{9,17},{17,9},{10,18},{18,10},{11,19},{19,11},{12,20... | collective-permute-start | bytes 49160 | tf_op jit(solution)/shard_map/ppermute | solution.py:382
  18.2 3.1 %collective-permute-start.6 = (f32[72,512]{1,0:T(8,128)S(1)}, f32[72,512]{1,0:T(8,128)S(1)}, u32[]{:S(2)}, u32[]{:S(2)}) collective-permute-start(f32[72,512]{1,0:T(8,128)S(1)} %collective-permute-done.3.refs_5_), channel_id=1, source_target_pairs={{0,1},{1,0},{2,3},{3,2},{4,5},{5,4},{6,7},{7,6},{8,9},{9,8},{10,11... | collective-permute-start | bytes 442376 | tf_op jit(solution)/shard_map/ppermute | solution.py:386
  20.3 1.4 %collective-permute-start.7 = (f32[72,512]{1,0:T(8,128)S(1)}, f32[72,512]{1,0:T(8,128)S(1)}, u32[]{:S(2)}, u32[]{:S(2)}) collective-permute-start(f32[72,512]{1,0:T(8,128)S(1)} %collective-permute-done.4.refs_4_), channel_id=1, source_target_pairs={{0,1},{1,0},{2,3},{3,2},{4,5},{5,4},{6,7},{7,6},{8,9},{9,8},{10,11... | collective-permute-start | bytes 442376 | tf_op jit(solution)/shard_map/ppermute | solution.py:386
  20.4 1.5 %collective-permute-start.8 = (f32[72,512]{1,0:T(8,128)S(1)}, f32[72,512]{1,0:T(8,128)S(1)}, u32[]{:S(2)}, u32[]{:S(2)}) collective-permute-start(f32[72,512]{1,0:T(8,128)S(1)} %collective-permute-done.5.refs_6_), channel_id=1, source_target_pairs={{0,1},{1,0},{2,3},{3,2},{4,5},{5,4},{6,7},{7,6},{8,9},{9,8},{10,11... | collective-permute-start | bytes 442376 | tf_op jit(solution)/shard_map/ppermute | solution.py:386
  31.8 9.6 %collective-permute-start.10 = (f32[64,512]{1,0:T(8,128)S(1)}, f32[64,512]{1,0:T(8,128)S(1)}, u32[]{:S(2)}, u32[]{:S(2)}) collective-permute-start(f32[64,512]{1,0:T(8,128)S(1)} %get-tuple-element.50), channel_id=1, source_target_pairs={{0,8},{16,24},{8,0},{24,16},{1,9},{17,25},{9,1},{25,17},{2,10},{18... | collective-permute-start | bytes 393224 | tf_op jit(solution)/shard_map/ppermute | solution.py:382
  31.9 9.5 %collective-permute-start.9 = (f32[64,512]{1,0:T(8,128)S(1)}, f32[64,512]{1,0:T(8,128)S(1)}, u32[]{:S(2)}, u32[]{:S(2)}) collective-permute-start(f32[64,512]{1,0:T(8,128)S(1)} %get-tuple-element.49), channel_id=1, source_target_pairs={{8,16},{16,8},{9,17},{17,9},{10,18},{18,10},{11,19},{19,11},{12,20... | collective-permute-start | bytes 393224 | tf_op jit(solution)/shard_map/ppermute | solution.py:382

commit v3 on v2

--- a/solution.py
+++ b/solution.py
@@ -11,6 +11,7 @@
 BLOCK = 256
 STRIP = 16
 UNROLL = 2
+COLS = 1 << 13
 FILL = 16
 FILL_LAST = 17
 VMEM_LIMIT = 48 * 1024 * 1024
@@ -82,31 +83,28 @@
         spec[k] for k in ("blocks", "first_block", "width", "groups", "outs", "part")
     )
     left, across, acc, points = ref["left"], ref["across"], ref["acc"], ref["points"]
-    plan, factor = ref["plan"], ref["factor"]
+    plan = ref["plan"]
+    bounds = plan.shape[0] - 2
     own_points = ref["own_points"]
     even = lax.rem(lax.axis_index("band"), 2) == 0
     base = acc.shape[1]
     half = base // 2
     spans = [slice(r * BLOCK, (r + 1) * BLOCK) for r in range(2)]
 
-    copies = []
     if part != "tail":
-        tables, sem = ref["tables"], ref["sem"]
-        lanes = tables.shape[2]
-        sources = [ref["col", s].at[base : base + EXTRA, 0:lanes] for s in range(blocks)]
-        sources.append(own_points.at[:, 0:lanes])
+        tables, counts, sem = ref["tables"], ref["counts"], ref["sem"]
+        lanes = tables.shape[1]
+        for s in range(blocks):
+            row = base + COUNT_ROW
+            counts[s : s + 1, :] = ref["col", s][row : row + 1, 0:lanes]
+        counts[blocks : blocks + 1, :] = own_points[COUNT_ROW : COUNT_ROW + 1, 0:lanes]
         if 1 in groups:
-            before = ref["before"]
-            before[...] = jnp.where(
-                even, ref["points", 1][:, 0:lanes], ref["points", 0][:, 0:lanes]
+            first, second = (
+                ref["points", k][COUNT_ROW : COUNT_ROW + 1, 0:lanes] for k in range(2)
             )
-            sources.append(before)
-        copies = [
-            pltpu.make_async_copy(source, tables.at[k], sem.at[k])
-            for k, source in enumerate(sources)
-        ]
-        for copy in copies:
-            copy.start()
+            counts[blocks + 1 : blocks + 2, :] = jnp.where(even, second, first)
+        copy = pltpu.make_async_copy(counts, tables, sem)
+        copy.start()
         for s in range(blocks):
             for h, span in enumerate(spans):
                 x = ref["col", s][0:base, span]
@@ -138,19 +136,19 @@
                 points[2 * k + r] = jnp.where(
                     even, ref["points", near][:, span], ref["points", far][:, span]
                 )
-    for copy in copies:
+    if part != "tail":
         copy.wait()
 
     if part == "tail":
-        first, end = ref["marks"][0], ref["marks"][1]
+        first, end = plan[bounds], plan[bounds + 1]
     else:
         me = lax.axis_index("dev")
         own_line, before_line = blocks, blocks + 1
 
         def add(total, s, h, row, value):
-            plan[total + 1] = (2 * s + h) * 8 + row
-            factor[total + 1] = value
-            return total + jnp.where(value > 0.0, 1, 0)
+            times = value.astype(jnp.int32)
+            plan[total + 1] = times * COLS + (2 * s + h) * 8 + row
+            return total + jnp.minimum(times, 1)
 
         def column_tiles(total, s, edge):
             if s + first_block == 0:
@@ -165,7 +163,7 @@
                         else:
                             line, row = own_line, 2 * groups.index(0) + r
                             lane = h * width + gap if gap >= 0 else r * width - gap
-                        total = add(total, s, h, row, tables[line, COUNT_ROW, lane])
+                        total = add(total, s, h, row, tables[line, lane])
                 return total
             ahead = jnp.bitwise_xor(me, s + first_block) - me
             after = ahead > 0
@@ -184,7 +182,7 @@
                         lane = h * width + gap
                     else:
                         lane = gap + jnp.where(first_is_col, h * width + r - h, r * width + h - r)
-                    total = add(total, s, h, rows + r, tables[line, COUNT_ROW, lane])
+                    total = add(total, s, h, rows + r, tables[line, lane])
             return total
 
         live = jnp.int32(0)
@@ -196,9 +194,7 @@
             for s in range(spec["own_done"], blocks):
                 live = column_tiles(live, s, False)
         plan[0] = 0
-        factor[0] = 0.0
         plan[live + 1] = 0
-        factor[live + 1] = 0.0
         first, end = 0, live
         if part == "head":
             band, bands = lax.axis_index("band"), lax.axis_size("band")
@@ -206,12 +202,13 @@
             fill = jnp.where(last, spec["fill_last"], spec["fill"])
             end = jnp.maximum(jnp.minimum(live, fill), live - spec["keep"])
             end = jnp.maximum(edge_tiles, end)
-            ref["marks"][0] = end
-            ref["marks"][1] = live
+            plan[bounds] = end
+            plan[bounds + 1] = live
 
     def entry_of(tile):
         entry = plan[tile + 1]
-        return lax.shift_right_logical(entry, 3), jnp.bitwise_and(entry, 7)
+        place = jnp.bitwise_and(entry, COLS - 1)
+        return lax.shift_right_logical(place, 3), jnp.bitwise_and(place, 7)
 
     def spread(tile, near_ref):
         col, _ = entry_of(tile)
@@ -241,7 +238,8 @@
         col, row = entry_of(tile)
         top = jnp.dot(left[col], hi_ref[...], preferred_element_type=jnp.float32)
         rest = jnp.dot(left[col, 0:base], lo_ref[...], preferred_element_type=jnp.float32)
-        acc[row] += factor[tile + 1] * (top[:base] + top[base:] + rest)
+        times = lax.shift_right_logical(plan[tile + 1], 13).astype(jnp.float32)
+        acc[row] += times * (top[:base] + top[base:] + rest)
 
     slots = [[ref[kind, k] for kind in ("hi", "lo", "near")] for k in range(2)]
 
@@ -314,9 +312,7 @@
         "left": ((2 * blocks, 2 * base, 2 * BLOCK), jnp.bfloat16, pltpu.VMEM),
         "across": ((-(-blocks // 8), BLOCK, 128), jnp.float32, pltpu.VMEM),
         "plan": ((tiles + 8,), jnp.int32, pltpu.SMEM),
-        "factor": ((tiles + 8,), jnp.float32, pltpu.SMEM),
     }
-    marks = {"marks": ((2,), jnp.int32, pltpu.SMEM)}
     args, outputs, scratch = {}, {}, {}
     args["own_points"] = (mine, vmem)
     for k, value in enumerate(points):
@@ -328,9 +324,9 @@
     for g in outs:
         outputs["sum", g] = ((base, own), jnp.float32, pltpu.VMEM)
     if part == "head":
-        outputs |= shared | marks
+        outputs |= shared
     elif part == "tail":
-        for name, (_, _, memory) in (shared | marks).items():
+        for name, (_, _, memory) in shared.items():
             args[name] = (ready[name], vmem if memory == pltpu.VMEM else smem)
     else:
         scratch |= shared
@@ -341,12 +337,13 @@
     scratch["points"] = ((n_rows, EXTRA, BLOCK), jnp.float32, pltpu.VMEM)
     scratch["acc"] = ((n_rows, base, BLOCK), jnp.float32, pltpu.VMEM)
     if part != "tail":
-        scratch["before"] = ((EXTRA, lanes), jnp.float32, pltpu.VMEM)
-        scratch["tables"] = ((blocks + 2, EXTRA, lanes), jnp.float32, pltpu.SMEM)
+        lines = -(-(blocks + 2) // 8) * 8
+        scratch["counts"] = ((lines, lanes), jnp.float32, pltpu.VMEM)
+        scratch["tables"] = ((lines, lanes), jnp.float32, pltpu.SMEM)
     scratch_shapes = [memory(shape, dtype) for shape, dtype, memory in scratch.values()]
     names = [*args, *outputs, *scratch]
     if part != "tail":
-        scratch_shapes.append(pltpu.SemaphoreType.DMA((blocks + 2,)))
+        scratch_shapes.append(pltpu.SemaphoreType.DMA)
         names.append("sem")
     spec = dict(
         blocks=blocks,

time: 41.7 us -> 41.4 us (level); the launches traced: 42.1 us -> 40.8 us
  starting transfers between devices: 14 us -> 13.3 us
  waiting for transfers between devices: 1.6 us -> 1.09 us
    ppermute x4, starting transfers between devices: 7.04 us -> 5.3 us  [paired(): return lax.ppermute(value, 'band', pairs + [(j, i) for i, j in pairs])]
    ppermute x7, starting transfers between devices: 6.92 us -> 8.01 us  [swapped(): lax.ppermute(value, axis, [(i, i ^ mask) for i in range(lax.axis_size(axi...]
    ppermute x4, waiting for transfers between devices: 0.53 us -> 0.01 us  [paired(): return lax.ppermute(value, 'band', pairs + [(j, i) for i, j in pairs])]
  transfers between devices with their start and end apart: 11 -> 11, of which waited for: 4 -> 3; matrix products, arithmetic and copies ran while one was open for 0% -> 0% of each run, Pallas kernels for 33% -> 34%
where the time goes in v3:
time: 41.4 us; the launch traced here: 40.8 us
  Pallas kernels  24.9 us (60%)
  starting transfers between devices  13.3 us (32%)
  waiting for transfers between devices  1.09 us (3%)
  between operations  0.78 us (2%)
  other arithmetic  0.69 us (2%)
    pallas_call x4, Pallas kernels, near_part(): pl.pallas_call(functools.partial(near_kernel, spec, names), out_shape=[ja...  23.7 us
    ppermute x7, starting transfers between devices, swapped(): lax.ppermute(value, axis, [(i, i ^ mask) for i in range(lax.axis_size(axi...  8.01 us
    ppermute x4, starting transfers between devices, paired(): return lax.ppermute(value, 'band', pairs + [(j, i) for i, j in pairs])  5.3 us
    pallas_call x1, Pallas kernels, body(): pl.pallas_call(functools.partial(pack_kernel, width), out_shape=[pltpu.VM...  1.19 us
    ppermute x7, waiting for transfers between devices, swapped(): lax.ppermute(value, axis, [(i, i ^ mask) for i in range(lax.axis_size(axi...  1.08 us
  transfers between devices with their start and end apart: 11, of which 3 were waited for; matrix products, arithmetic and copies ran while one was open for 0% of the time, Pallas kernels for 34%

profile of v3, /device:TPU:29, one launch (start us, length us, event | category | flops | bytes accessed | tf_op | source)
XLA Modules:
  0.0 40.8 jit_solution(91779710805088896)
XLA Ops:
  0.7 1.2 %shard_map.64 = (f32[72,512]{1,0:T(8,128)S(1)}, f32[8,512]{1,0:T(8,128)S(1)}) custom-call(f32[2,32,512]{2,1,0:T(8,128)} %drive.1, f32[3,512]{1,0:T(4,128)} %coords.1, s32[1,512]{1,0:T(1,128)} %bitcast.8, f32[1,4]{1,0:T(1,128)} %bitcast.9, s32[1,96]{1,0:T(1,128)} %bitcast.10, s32[1,1]{1,0:T(1,128)} %bitcast.6.pair_count), custom_call_target="tpu_custom_call" | custom-call | tf_op jit(solution)/shard_map/pallas_call | solution.py:392
  1.8 0.7 %collective-permute-start = (f32[72,512]{1,0:T(8,128)S(1)}, f32[72,512]{1,0:T(8,128)S(1)}, u32[]{:S(2)}, u32[]{:S(2)}) collective-permute-start(f32[72,512]{1,0:T(8,128)S(1)} %get-tuple-element.27.refs_1_.refs_3_), channel_id=1, source_target_pairs={{0,1},{1,0},{2,3},{3,2},{4,5},{5,4},{6,7},{7,6},{8,9},{9,8},{10,11... | collective-permute-start | bytes 442376 | tf_op jit(solution)/shard_map/ppermute | solution.py:383
  2.6 0.2 collective-permute-start.3
  2.8 0.1 collective-permute-start.4
  2.8 3.3 %collective-permute-start.5 = (f32[72,512]{1,0:T(8,128)S(1)}, f32[72,512]{1,0:T(8,128)S(1)}, u32[]{:S(2)}, u32[]{:S(2)}) collective-permute-start(f32[72,512]{1,0:T(8,128)S(1)} %get-tuple-element.27.refs_1_.refs_3_), channel_id=1, source_target_pairs={{0,6},{1,7},{2,4},{3,5},{4,2},{5,3},{6,0},{7,1},{8,14},{9,15},{10,... | collective-permute-start | bytes 442376 | tf_op jit(solution)/shard_map/ppermute | solution.py:383
  6.2 0.0 collective-permute-done.refs_2_.refs_4_
  6.2 1.2 %collective-permute-start.1 = (f32[8,512]{1,0:T(8,128)S(1)}, f32[8,512]{1,0:T(8,128)S(1)}, u32[]{:S(2)}, u32[]{:S(2)}) collective-permute-start(f32[8,512]{1,0:T(8,128)S(1)} %get-tuple-element.28.refs_0_), channel_id=1, source_target_pairs={{0,8},{16,24},{8,0},{24,16},{1,9},{17,25},{9,1},{25,17},{2,10},{18... | collective-permute-start | bytes 49160 | tf_op jit(solution)/shard_map/ppermute | solution.py:379
  7.4 2.1 %collective-permute-start.2 = (f32[8,512]{1,0:T(8,128)S(1)}, f32[8,512]{1,0:T(8,128)S(1)}, u32[]{:S(2)}, u32[]{:S(2)}) collective-permute-start(f32[8,512]{1,0:T(8,128)S(1)} %get-tuple-element.28.refs_0_), channel_id=1, source_target_pairs={{8,16},{16,8},{9,17},{17,9},{10,18},{18,10},{11,19},{19,11},{12,20... | collective-permute-start | bytes 49160 | tf_op jit(solution)/shard_map/ppermute | solution.py:379
  9.5 3.6 %shard_map.65.refs_6_ = f32[64,512]{1,0:T(8,128)S(1)} custom-call(f32[8,512]{1,0:T(8,128)S(1)} %get-tuple-element.28.refs_0_, f32[72,512]{1,0:T(8,128)S(1)} %get-tuple-element.27.refs_1_.refs_3_, f32[72,512]{1,0:T(8,128)S(1)} %collective-permute-done.refs_2_.refs_4_), custom_call_target="tpu_custom_call" | custom-call | flops 402653184 | bytes 655360 | tf_op jit(solution)/shard_map/pallas_call | solution.py:360
  13.1 0.0 collective-permute-done.1.refs_1_
  13.1 0.0 collective-permute-done.2.refs_2_
  13.1 0.0 collective-permute-done.3.refs_5_
  13.1 4.5 %shard_map.66 = (f32[64,512]{1,0:T(8,128)S(1)}, f32[64,512]{1,0:T(8,128)S(1)}, f32[64,512]{1,0:T(8,128)S(1)}) custom-call(f32[8,512]{1,0:T(8,128)S(1)} %get-tuple-element.28.refs_0_, f32[8,512]{1,0:T(8,128)S(1)} %collective-permute-done.1.refs_1_, f32[8,512]{1,0:T(8,128)S(1)} %collective-permute-done.2.refs_2_, ...), custom_call_target="tpu_custom_call" | custom-call | flops 1811939328 | bytes 786432 | tf_op jit(solution)/shard_map/pallas_call | solution.py:360
  17.7 0.0 collective-permute-done.4.refs_4_
  17.7 0.0 collective-permute-done.5.refs_6_
  17.7 3.2 %collective-permute-start.6 = (f32[72,512]{1,0:T(8,128)S(1)}, f32[72,512]{1,0:T(8,128)S(1)}, u32[]{:S(2)}, u32[]{:S(2)}) collective-permute-start(f32[72,512]{1,0:T(8,128)S(1)} %collective-permute-done.3.refs_5_), channel_id=1, source_target_pairs={{0,1},{1,0},{2,3},{3,2},{4,5},{5,4},{6,7},{7,6},{8,9},{9,8},{10,11... | collective-permute-start | bytes 442376 | tf_op jit(solution)/shard_map/ppermute | solution.py:383
  20.9 0.1 collective-permute-start.7
  21.0 0.4 %collective-permute-start.8 = (f32[72,512]{1,0:T(8,128)S(1)}, f32[72,512]{1,0:T(8,128)S(1)}, u32[]{:S(2)}, u32[]{:S(2)}) collective-permute-start(f32[72,512]{1,0:T(8,128)S(1)} %collective-permute-done.5.refs_6_), channel_id=1, source_target_pairs={{0,1},{1,0},{2,3},{3,2},{4,5},{5,4},{6,7},{7,6},{8,9},{9,8},{10,11... | collective-permute-start | bytes 442376 | tf_op jit(solution)/shard_map/ppermute | solution.py:383
  21.4 0.5 %collective-permute-done.6.refs_3_ = f32[72,512]{1,0:T(8,128)S(1)} collective-permute-done((f32[72,512]{1,0:T(8,128)S(1)}, f32[72,512]{1,0:T(8,128)S(1)}, u32[]{:S(2)}, u32[]{:S(2)}) %collective-permute-start.6) | collective-permute-done | bytes 147488 | tf_op jit(solution)/shard_map/ppermute | solution.py:383
  21.9 0.4 collective-permute-done.7.refs_5_
  22.2 0.2 collective-permute-done.8.refs_7_
  22.5 9.7 %shard_map.67 = (f32[64,512]{1,0:T(8,128)S(1)}, f32[64,512]{1,0:T(8,128)S(1)}, f32[64,512]{1,0:T(8,128)S(1)}, bf16[10,128,512]{2,1,0:T(8,128)(2,1)S(1)}, f32[1,256,128]{2,1,0:T(8,128)S(1)}, /*index=5*/s32[68]{0:T(128)S(1)}) custom-call(f32[8,512]{1,0:T(8,128)S(1)} %get-tuple-element.28.refs_0_, f32[8,512]{1,0:T(8,128)S(1)} %collective-permute-done.1.refs_1_, ...), custom_call_target="tpu_custom_call" | custom-call | flops 3019898880 | bytes 1048576 | tf_op jit(solution)/shard_map/pallas_call | solution.py:360
  32.2 0.1 collective-permute-start.10
  32.3 1.9 %collective-permute-start.9 = (f32[64,512]{1,0:T(8,128)S(1)}, f32[64,512]{1,0:T(8,128)S(1)}, u32[]{:S(2)}, u32[]{:S(2)}) collective-permute-start(f32[64,512]{1,0:T(8,128)S(1)} %get-tuple-element.45), channel_id=1, source_target_pairs={{8,16},{16,8},{9,17},{17,9},{10,18},{18,10},{11,19},{19,11},{12,20... | collective-permute-start | bytes 393224 | tf_op jit(solution)/shard_map/ppermute | solution.py:379
  34.2 5.8 %shard_map.68 = f32[64,512]{1,0:T(8,128)S(1)} custom-call(f32[8,512]{1,0:T(8,128)S(1)} %get-tuple-element.28.refs_0_, f32[64,512]{1,0:T(8,128)S(1)} %get-tuple-element.41.refs_1_, bf16[10,128,512]{2,1,0:T(8,128)(2,1)S(1)} %get-tuple-element.42.refs_2_, f32[1,256,128]{2,1,0:T(8,128)S(1)} %get-tuple-element.43.refs_3_, s32[68]{0:T(128)S(1)} %get-tuple-element.44.refs_4_), custom_call_target="tpu_custom_call" | custom-call | flops 3019898880 | bytes 1048576 | tf_op jit(solution)/shard_map/pallas_call | solution.py:360
  40.1 0.0 collective-permute-done.10
  40.1 0.0 collective-permute-done.9
  40.1 0.7 %add_multiply_fusion = f32[64,512]{1,0:T(8,128)} fusion(f32[64,512]{1,0:T(8,128)S(1)} %shard_map.68, f32[64,512]{1,0:T(8,128)S(1)} %collective-permute-done.9, f32[64,512]{1,0:T(8,128)S(1)} %collective-permute-done.10, f32[512]{0:T(512)S(1)} %bitcast.7), kind=kLoop, calls=%fused_computation | loop fusion | flops 98304 | bytes 526336 | tf_op jit(solution)/shard_map/mul | solution.py:428
  (1 shorter events, 0.0 us)
Async XLA Ops:
  1.8 4.3 %collective-permute-start = (f32[72,512]{1,0:T(8,128)S(1)}, f32[72,512]{1,0:T(8,128)S(1)}, u32[]{:S(2)}, u32[]{:S(2)}) collective-permute-start(f32[72,512]{1,0:T(8,128)S(1)} %get-tuple-element.27.refs_1_.refs_3_), channel_id=1, source_target_pairs={{0,1},{1,0},{2,3},{3,2},{4,5},{5,4},{6,7},{7,6},{8,9},{9,8},{10,11... | collective-permute-start | bytes 442376 | tf_op jit(solution)/shard_map/ppermute | solution.py:383
  2.6 10.5 %collective-permute-start.3 = (f32[72,512]{1,0:T(8,128)S(1)}, f32[72,512]{1,0:T(8,128)S(1)}, u32[]{:S(2)}, u32[]{:S(2)}) collective-permute-start(f32[72,512]{1,0:T(8,128)S(1)} %get-tuple-element.27.refs_1_.refs_3_), channel_id=1, source_target_pairs={{0,2},{1,3},{2,0},{3,1},{4,6},{5,7},{6,4},{7,5},{8,10},{9,11},{10,... | collective-permute-start | bytes 442376 | tf_op jit(solution)/shard_map/ppermute | solution.py:383
  2.8 14.9 %collective-permute-start.4 = (f32[72,512]{1,0:T(8,128)S(1)}, f32[72,512]{1,0:T(8,128)S(1)}, u32[]{:S(2)}, u32[]{:S(2)}) collective-permute-start(f32[72,512]{1,0:T(8,128)S(1)} %get-tuple-element.27.refs_1_.refs_3_), channel_id=1, source_target_pairs={{0,4},{1,5},{2,6},{3,7},{4,0},{5,1},{6,2},{7,3},{8,12},{9,13},{10,... | collective-permute-start | bytes 442376 | tf_op jit(solution)/shard_map/ppermute | solution.py:383
  2.8 14.8 %collective-permute-start.5 = (f32[72,512]{1,0:T(8,128)S(1)}, f32[72,512]{1,0:T(8,128)S(1)}, u32[]{:S(2)}, u32[]{:S(2)}) collective-permute-start(f32[72,512]{1,0:T(8,128)S(1)} %get-tuple-element.27.refs_1_.refs_3_), channel_id=1, source_target_pairs={{0,6},{1,7},{2,4},{3,5},{4,2},{5,3},{6,0},{7,1},{8,14},{9,15},{10,... | collective-permute-start | bytes 442376 | tf_op jit(solution)/shard_map/ppermute | solution.py:383
  6.2 6.9 %collective-permute-start.1 = (f32[8,512]{1,0:T(8,128)S(1)}, f32[8,512]{1,0:T(8,128)S(1)}, u32[]{:S(2)}, u32[]{:S(2)}) collective-permute-start(f32[8,512]{1,0:T(8,128)S(1)} %get-tuple-element.28.refs_0_), channel_id=1, source_target_pairs={{0,8},{16,24},{8,0},{24,16},{1,9},{17,25},{9,1},{25,17},{2,10},{18... | collective-permute-start | bytes 49160 | tf_op jit(solution)/shard_map/ppermute | solution.py:379
  7.4 5.7 %collective-permute-start.2 = (f32[8,512]{1,0:T(8,128)S(1)}, f32[8,512]{1,0:T(8,128)S(1)}, u32[]{:S(2)}, u32[]{:S(2)}) collective-permute-start(f32[8,512]{1,0:T(8,128)S(1)} %get-tuple-element.28.refs_0_), channel_id=1, source_target_pairs={{8,16},{16,8},{9,17},{17,9},{10,18},{18,10},{11,19},{19,11},{12,20... | collective-permute-start | bytes 49160 | tf_op jit(solution)/shard_map/ppermute | solution.py:379
  17.7 4.2 %collective-permute-start.6 = (f32[72,512]{1,0:T(8,128)S(1)}, f32[72,512]{1,0:T(8,128)S(1)}, u32[]{:S(2)}, u32[]{:S(2)}) collective-permute-start(f32[72,512]{1,0:T(8,128)S(1)} %collective-permute-done.3.refs_5_), channel_id=1, source_target_pairs={{0,1},{1,0},{2,3},{3,2},{4,5},{5,4},{6,7},{7,6},{8,9},{9,8},{10,11... | collective-permute-start | bytes 442376 | tf_op jit(solution)/shard_map/ppermute | solution.py:383
  20.9 1.4 %collective-permute-start.7 = (f32[72,512]{1,0:T(8,128)S(1)}, f32[72,512]{1,0:T(8,128)S(1)}, u32[]{:S(2)}, u32[]{:S(2)}) collective-permute-start(f32[72,512]{1,0:T(8,128)S(1)} %collective-permute-done.4.refs_4_), channel_id=1, source_target_pairs={{0,1},{1,0},{2,3},{3,2},{4,5},{5,4},{6,7},{7,6},{8,9},{9,8},{10,11... | collective-permute-start | bytes 442376 | tf_op jit(solution)/shard_map/ppermute | solution.py:383
  21.0 1.5 %collective-permute-start.8 = (f32[72,512]{1,0:T(8,128)S(1)}, f32[72,512]{1,0:T(8,128)S(1)}, u32[]{:S(2)}, u32[]{:S(2)}) collective-permute-start(f32[72,512]{1,0:T(8,128)S(1)} %collective-permute-done.5.refs_6_), channel_id=1, source_target_pairs={{0,1},{1,0},{2,3},{3,2},{4,5},{5,4},{6,7},{7,6},{8,9},{9,8},{10,11... | collective-permute-start | bytes 442376 | tf_op jit(solution)/shard_map/ppermute | solution.py:383
  32.2 7.9 %collective-permute-start.10 = (f32[64,512]{1,0:T(8,128)S(1)}, f32[64,512]{1,0:T(8,128)S(1)}, u32[]{:S(2)}, u32[]{:S(2)}) collective-permute-start(f32[64,512]{1,0:T(8,128)S(1)} %get-tuple-element.46), channel_id=1, source_target_pairs={{0,8},{16,24},{8,0},{24,16},{1,9},{17,25},{9,1},{25,17},{2,10},{18... | collective-permute-start | bytes 393224 | tf_op jit(solution)/shard_map/ppermute | solution.py:379
  32.3 7.8 %collective-permute-start.9 = (f32[64,512]{1,0:T(8,128)S(1)}, f32[64,512]{1,0:T(8,128)S(1)}, u32[]{:S(2)}, u32[]{:S(2)}) collective-permute-start(f32[64,512]{1,0:T(8,128)S(1)} %get-tuple-element.45), channel_id=1, source_target_pairs={{8,16},{16,8},{9,17},{17,9},{10,18},{18,10},{11,19},{19,11},{12,20... | collective-permute-start | bytes 393224 | tf_op jit(solution)/shard_map/ppermute | solution.py:379

commit v4 on v3

--- a/solution.py
+++ b/solution.py
@@ -105,7 +105,7 @@
             counts[blocks + 1 : blocks + 2, :] = jnp.where(even, second, first)
         copy = pltpu.make_async_copy(counts, tables, sem)
         copy.start()
-        for s in range(blocks):
+        def operands(s):
             for h, span in enumerate(spans):
                 x = ref["col", s][0:base, span]
                 turned = jnp.concatenate([-2.0 * x[half:], 2.0 * x[:half]], 0)
@@ -115,6 +115,9 @@
                 left[2 * s + h, base : 2 * base, :] = (wide - hi.astype(jnp.float32)).astype(
                     jnp.bfloat16
                 )
+
+        for s in range(blocks // 3):
+            operands(s)
         lines = [ref["col", s][base : base + EXTRA, span] for s in range(blocks) for span in spans]
         for k in range(across.shape[0]):
             some = lines[16 * k : 16 * (k + 1)]
@@ -138,6 +141,8 @@
                 )
     if part != "tail":
         copy.wait()
+        for s in range(blocks // 3, blocks):
+            operands(s)
 
     if part == "tail":
         first, end = plan[bounds], plan[bounds + 1]

time: 41.4 us -> 41.4 us (level)
  the two profiles are of different devices: /device:TPU:29 before, /device:TPU:18 now
where the time goes in v4:
time: 41.4 us; the launch traced here: 41.3 us
  Pallas kernels  22.3 us (54%)
  starting transfers between devices  14 us (34%)
  waiting for transfers between devices  3.59 us (9%)
  between operations  0.78 us (2%)
  other arithmetic  0.69 us (2%)
    pallas_call x4, Pallas kernels, near_part(): pl.pallas_call(functools.partial(near_kernel, spec, names), out_shape=[ja...  21.1 us
    ppermute x4, starting transfers between devices, paired(): return lax.ppermute(value, 'band', pairs + [(j, i) for i, j in pairs])  9.83 us
    ppermute x7, starting transfers between devices, swapped(): lax.ppermute(value, axis, [(i, i ^ mask) for i in range(lax.axis_size(axi...  4.14 us
    ppermute x7, waiting for transfers between devices, swapped(): lax.ppermute(value, axis, [(i, i ^ mask) for i in range(lax.axis_size(axi...  3.58 us
    pallas_call x1, Pallas kernels, body(): pl.pallas_call(functools.partial(pack_kernel, width), out_shape=[pltpu.VM...  1.19 us
  transfers between devices with their start and end apart: 11, of which 4 were waited for; matrix products, arithmetic and copies ran while one was open for 0% of the time, Pallas kernels for 29%

profile of v4, /device:TPU:18, one launch (start us, length us, event | category | flops | bytes accessed | tf_op | source)
XLA Modules:
  0.0 41.3 jit_solution(14248549571662733790)
XLA Ops:
  0.7 1.2 %shard_map.64 = (f32[72,512]{1,0:T(8,128)S(1)}, f32[8,512]{1,0:T(8,128)S(1)}) custom-call(f32[2,32,512]{2,1,0:T(8,128)} %drive.1, f32[3,512]{1,0:T(4,128)} %coords.1, s32[1,512]{1,0:T(1,128)} %bitcast.8, f32[1,4]{1,0:T(1,128)} %bitcast.9, s32[1,96]{1,0:T(1,128)} %bitcast.10, s32[1,1]{1,0:T(1,128)} %bitcast.6.pair_count), custom_call_target="tpu_custom_call" | custom-call | tf_op jit(solution)/shard_map/pallas_call | solution.py:397
  1.8 0.1 collective-permute-start
  1.9 1.6 %collective-permute-start.3 = (f32[72,512]{1,0:T(8,128)S(1)}, f32[72,512]{1,0:T(8,128)S(1)}, u32[]{:S(2)}, u32[]{:S(2)}) collective-permute-start(f32[72,512]{1,0:T(8,128)S(1)} %get-tuple-element.27.refs_1_.refs_3_), channel_id=1, source_target_pairs={{0,2},{1,3},{2,0},{3,1},{4,6},{5,7},{6,4},{7,5},{8,10},{9,11},{10,... | collective-permute-start | bytes 442376 | tf_op jit(solution)/shard_map/ppermute | solution.py:388
  3.6 0.3 collective-permute-start.4
  3.9 1.6 %collective-permute-start.5 = (f32[72,512]{1,0:T(8,128)S(1)}, f32[72,512]{1,0:T(8,128)S(1)}, u32[]{:S(2)}, u32[]{:S(2)}) collective-permute-start(f32[72,512]{1,0:T(8,128)S(1)} %get-tuple-element.27.refs_1_.refs_3_), channel_id=1, source_target_pairs={{0,6},{1,7},{2,4},{3,5},{4,2},{5,3},{6,0},{7,1},{8,14},{9,15},{10,... | collective-permute-start | bytes 442376 | tf_op jit(solution)/shard_map/ppermute | solution.py:388
  5.5 0.0 collective-permute-done.refs_2_.refs_4_
  5.5 0.5 %collective-permute-start.1 = (f32[8,512]{1,0:T(8,128)S(1)}, f32[8,512]{1,0:T(8,128)S(1)}, u32[]{:S(2)}, u32[]{:S(2)}) collective-permute-start(f32[8,512]{1,0:T(8,128)S(1)} %get-tuple-element.28.refs_0_), channel_id=1, source_target_pairs={{0,8},{16,24},{8,0},{24,16},{1,9},{17,25},{9,1},{25,17},{2,10},{18... | collective-permute-start | bytes 49160 | tf_op jit(solution)/shard_map/ppermute | solution.py:384
  6.0 4.3 %collective-permute-start.2 = (f32[8,512]{1,0:T(8,128)S(1)}, f32[8,512]{1,0:T(8,128)S(1)}, u32[]{:S(2)}, u32[]{:S(2)}) collective-permute-start(f32[8,512]{1,0:T(8,128)S(1)} %get-tuple-element.28.refs_0_), channel_id=1, source_target_pairs={{8,16},{16,8},{9,17},{17,9},{10,18},{18,10},{11,19},{19,11},{12,20... | collective-permute-start | bytes 49160 | tf_op jit(solution)/shard_map/ppermute | solution.py:384
  10.4 2.9 %shard_map.65.refs_6_ = f32[64,512]{1,0:T(8,128)S(1)} custom-call(f32[8,512]{1,0:T(8,128)S(1)} %get-tuple-element.28.refs_0_, f32[72,512]{1,0:T(8,128)S(1)} %get-tuple-element.27.refs_1_.refs_3_, f32[72,512]{1,0:T(8,128)S(1)} %collective-permute-done.refs_2_.refs_4_), custom_call_target="tpu_custom_call" | custom-call | flops 402653184 | bytes 655360 | tf_op jit(solution)/shard_map/pallas_call | solution.py:365
  13.2 0.0 collective-permute-done.1.refs_1_
  13.3 0.0 collective-permute-done.2.refs_2_
  13.3 0.0 collective-permute-done.3.refs_5_
  13.3 3.4 %shard_map.66 = (f32[64,512]{1,0:T(8,128)S(1)}, f32[64,512]{1,0:T(8,128)S(1)}, f32[64,512]{1,0:T(8,128)S(1)}) custom-call(f32[8,512]{1,0:T(8,128)S(1)} %get-tuple-element.28.refs_0_, f32[8,512]{1,0:T(8,128)S(1)} %collective-permute-done.1.refs_1_, f32[8,512]{1,0:T(8,128)S(1)} %collective-permute-done.2.refs_2_, ...), custom_call_target="tpu_custom_call" | custom-call | flops 1811939328 | bytes 786432 | tf_op jit(solution)/shard_map/pallas_call | solution.py:365
  16.7 0.0 collective-permute-done.4.refs_4_
  16.7 2.2 %collective-permute-done.5.refs_6_ = f32[72,512]{1,0:T(8,128)S(1)} collective-permute-done((f32[72,512]{1,0:T(8,128)S(1)}, f32[72,512]{1,0:T(8,128)S(1)}, u32[]{:S(2)}, u32[]{:S(2)}) %collective-permute-start.5) | collective-permute-done | bytes 147488 | tf_op jit(solution)/shard_map/ppermute | solution.py:388
  18.9 0.0 collective-permute-start.6
  18.9 0.5 %collective-permute-start.7 = (f32[72,512]{1,0:T(8,128)S(1)}, f32[72,512]{1,0:T(8,128)S(1)}, u32[]{:S(2)}, u32[]{:S(2)}) collective-permute-start(f32[72,512]{1,0:T(8,128)S(1)} %collective-permute-done.4.refs_4_), channel_id=1, source_target_pairs={{0,1},{1,0},{2,3},{3,2},{4,5},{5,4},{6,7},{7,6},{8,9},{9,8},{10,11... | collective-permute-start | bytes 442376 | tf_op jit(solution)/shard_map/ppermute | solution.py:388
  19.4 0.0 collective-permute-start.8
  19.4 0.9 %collective-permute-done.6.refs_3_ = f32[72,512]{1,0:T(8,128)S(1)} collective-permute-done((f32[72,512]{1,0:T(8,128)S(1)}, f32[72,512]{1,0:T(8,128)S(1)}, u32[]{:S(2)}, u32[]{:S(2)}) %collective-permute-start.6) | collective-permute-done | bytes 147488 | tf_op jit(solution)/shard_map/ppermute | solution.py:388
  20.3 0.2 collective-permute-done.7.refs_5_
  20.5 0.3 collective-permute-done.8.refs_7_
  20.8 9.0 %shard_map.67 = (f32[64,512]{1,0:T(8,128)S(1)}, f32[64,512]{1,0:T(8,128)S(1)}, f32[64,512]{1,0:T(8,128)S(1)}, bf16[10,128,512]{2,1,0:T(8,128)(2,1)S(1)}, f32[1,256,128]{2,1,0:T(8,128)S(1)}, /*index=5*/s32[68]{0:T(128)S(1)}) custom-call(f32[8,512]{1,0:T(8,128)S(1)} %get-tuple-element.28.refs_0_, f32[8,512]{1,0:T(8,128)S(1)} %collective-permute-done.1.refs_1_, ...), custom_call_target="tpu_custom_call" | custom-call | flops 3019898880 | bytes 1048576 | tf_op jit(solution)/shard_map/pallas_call | solution.py:365
  29.8 0.1 collective-permute-start.10
  29.9 4.9 %collective-permute-start.9 = (f32[64,512]{1,0:T(8,128)S(1)}, f32[64,512]{1,0:T(8,128)S(1)}, u32[]{:S(2)}, u32[]{:S(2)}) collective-permute-start(f32[64,512]{1,0:T(8,128)S(1)} %get-tuple-element.45), channel_id=1, source_target_pairs={{8,16},{16,8},{9,17},{17,9},{10,18},{18,10},{11,19},{19,11},{12,20... | collective-permute-start | bytes 393224 | tf_op jit(solution)/shard_map/ppermute | solution.py:384
  34.8 5.9 %shard_map.68 = f32[64,512]{1,0:T(8,128)S(1)} custom-call(f32[8,512]{1,0:T(8,128)S(1)} %get-tuple-element.28.refs_0_, f32[64,512]{1,0:T(8,128)S(1)} %get-tuple-element.41.refs_1_, bf16[10,128,512]{2,1,0:T(8,128)(2,1)S(1)} %get-tuple-element.42.refs_2_, f32[1,256,128]{2,1,0:T(8,128)S(1)} %get-tuple-element.43.refs_3_, s32[68]{0:T(128)S(1)} %get-tuple-element.44.refs_4_), custom_call_target="tpu_custom_call" | custom-call | flops 3019898880 | bytes 1048576 | tf_op jit(solution)/shard_map/pallas_call | solution.py:365
  40.6 0.0 collective-permute-done.10
  40.6 0.0 collective-permute-done.9
  40.6 0.7 %add_multiply_fusion = f32[64,512]{1,0:T(8,128)} fusion(f32[64,512]{1,0:T(8,128)S(1)} %shard_map.68, f32[64,512]{1,0:T(8,128)S(1)} %collective-permute-done.9, f32[64,512]{1,0:T(8,128)S(1)} %collective-permute-done.10, f32[512]{0:T(512)S(1)} %bitcast.7), kind=kLoop, calls=%fused_computation | loop fusion | flops 98304 | bytes 526336 | tf_op jit(solution)/shard_map/mul | solution.py:433
  (1 shorter events, 0.0 us)
Async XLA Ops:
  1.8 3.6 %collective-permute-start = (f32[72,512]{1,0:T(8,128)S(1)}, f32[72,512]{1,0:T(8,128)S(1)}, u32[]{:S(2)}, u32[]{:S(2)}) collective-permute-start(f32[72,512]{1,0:T(8,128)S(1)} %get-tuple-element.27.refs_1_.refs_3_), channel_id=1, source_target_pairs={{0,1},{1,0},{2,3},{3,2},{4,5},{5,4},{6,7},{7,6},{8,9},{9,8},{10,11... | collective-permute-start | bytes 442376 | tf_op jit(solution)/shard_map/ppermute | solution.py:388
  1.9 11.3 %collective-permute-start.3 = (f32[72,512]{1,0:T(8,128)S(1)}, f32[72,512]{1,0:T(8,128)S(1)}, u32[]{:S(2)}, u32[]{:S(2)}) collective-permute-start(f32[72,512]{1,0:T(8,128)S(1)} %get-tuple-element.27.refs_1_.refs_3_), channel_id=1, source_target_pairs={{0,2},{1,3},{2,0},{3,1},{4,6},{5,7},{6,4},{7,5},{8,10},{9,11},{10,... | collective-permute-start | bytes 442376 | tf_op jit(solution)/shard_map/ppermute | solution.py:388
  3.6 13.1 %collective-permute-start.4 = (f32[72,512]{1,0:T(8,128)S(1)}, f32[72,512]{1,0:T(8,128)S(1)}, u32[]{:S(2)}, u32[]{:S(2)}) collective-permute-start(f32[72,512]{1,0:T(8,128)S(1)} %get-tuple-element.27.refs_1_.refs_3_), channel_id=1, source_target_pairs={{0,4},{1,5},{2,6},{3,7},{4,0},{5,1},{6,2},{7,3},{8,12},{9,13},{10,... | collective-permute-start | bytes 442376 | tf_op jit(solution)/shard_map/ppermute | solution.py:388
  3.9 15.0 %collective-permute-start.5 = (f32[72,512]{1,0:T(8,128)S(1)}, f32[72,512]{1,0:T(8,128)S(1)}, u32[]{:S(2)}, u32[]{:S(2)}) collective-permute-start(f32[72,512]{1,0:T(8,128)S(1)} %get-tuple-element.27.refs_1_.refs_3_), channel_id=1, source_target_pairs={{0,6},{1,7},{2,4},{3,5},{4,2},{5,3},{6,0},{7,1},{8,14},{9,15},{10,... | collective-permute-start | bytes 442376 | tf_op jit(solution)/shard_map/ppermute | solution.py:388
  5.5 7.8 %collective-permute-start.1 = (f32[8,512]{1,0:T(8,128)S(1)}, f32[8,512]{1,0:T(8,128)S(1)}, u32[]{:S(2)}, u32[]{:S(2)}) collective-permute-start(f32[8,512]{1,0:T(8,128)S(1)} %get-tuple-element.28.refs_0_), channel_id=1, source_target_pairs={{0,8},{16,24},{8,0},{24,16},{1,9},{17,25},{9,1},{25,17},{2,10},{18... | collective-permute-start | bytes 49160 | tf_op jit(solution)/shard_map/ppermute | solution.py:384
  6.0 7.2 %collective-permute-start.2 = (f32[8,512]{1,0:T(8,128)S(1)}, f32[8,512]{1,0:T(8,128)S(1)}, u32[]{:S(2)}, u32[]{:S(2)}) collective-permute-start(f32[8,512]{1,0:T(8,128)S(1)} %get-tuple-element.28.refs_0_), channel_id=1, source_target_pairs={{8,16},{16,8},{9,17},{17,9},{10,18},{18,10},{11,19},{19,11},{12,20... | collective-permute-start | bytes 49160 | tf_op jit(solution)/shard_map/ppermute | solution.py:384
  18.9 1.4 %collective-permute-start.6 = (f32[72,512]{1,0:T(8,128)S(1)}, f32[72,512]{1,0:T(8,128)S(1)}, u32[]{:S(2)}, u32[]{:S(2)}) collective-permute-start(f32[72,512]{1,0:T(8,128)S(1)} %collective-permute-done.3.refs_5_), channel_id=1, source_target_pairs={{0,1},{1,0},{2,3},{3,2},{4,5},{5,4},{6,7},{7,6},{8,9},{9,8},{10,11... | collective-permute-start | bytes 442376 | tf_op jit(solution)/shard_map/ppermute | solution.py:388
  18.9 1.6 %collective-permute-start.7 = (f32[72,512]{1,0:T(8,128)S(1)}, f32[72,512]{1,0:T(8,128)S(1)}, u32[]{:S(2)}, u32[]{:S(2)}) collective-permute-start(f32[72,512]{1,0:T(8,128)S(1)} %collective-permute-done.4.refs_4_), channel_id=1, source_target_pairs={{0,1},{1,0},{2,3},{3,2},{4,5},{5,4},{6,7},{7,6},{8,9},{9,8},{10,11... | collective-permute-start | bytes 442376 | tf_op jit(solution)/shard_map/ppermute | solution.py:388
  19.4 1.4 %collective-permute-start.8 = (f32[72,512]{1,0:T(8,128)S(1)}, f32[72,512]{1,0:T(8,128)S(1)}, u32[]{:S(2)}, u32[]{:S(2)}) collective-permute-start(f32[72,512]{1,0:T(8,128)S(1)} %collective-permute-done.5.refs_6_), channel_id=1, source_target_pairs={{0,1},{1,0},{2,3},{3,2},{4,5},{5,4},{6,7},{7,6},{8,9},{9,8},{10,11... | collective-permute-start | bytes 442376 | tf_op jit(solution)/shard_map/ppermute | solution.py:388
  29.8 10.8 %collective-permute-start.10 = (f32[64,512]{1,0:T(8,128)S(1)}, f32[64,512]{1,0:T(8,128)S(1)}, u32[]{:S(2)}, u32[]{:S(2)}) collective-permute-start(f32[64,512]{1,0:T(8,128)S(1)} %get-tuple-element.46), channel_id=1, source_target_pairs={{0,8},{16,24},{8,0},{24,16},{1,9},{17,25},{9,1},{25,17},{2,10},{18... | collective-permute-start | bytes 393224 | tf_op jit(solution)/shard_map/ppermute | solution.py:384
  29.9 10.8 %collective-permute-start.9 = (f32[64,512]{1,0:T(8,128)S(1)}, f32[64,512]{1,0:T(8,128)S(1)}, u32[]{:S(2)}, u32[]{:S(2)}) collective-permute-start(f32[64,512]{1,0:T(8,128)S(1)} %get-tuple-element.45), channel_id=1, source_target_pairs={{8,16},{16,8},{9,17},{17,9},{10,18},{18,10},{11,19},{19,11},{12,20... | collective-permute-start | bytes 393224 | tf_op jit(solution)/shard_map/ppermute | solution.py:384
